TPU v7x, 32 devices: a whole 2x2x4 slice. The times are simulated.
32 devices in a mesh: expert: 8 (over z, y), tensor: 4 (over x, core).
Axes of the slice: x: 2, y: 2, z: 4, core: 2. Of those that a mesh axis runs over, the one named last changes fastest.
Arguments:
- tokens: bfloat16 [1024, 768], P('expert', 'tensor'), may hold values from -6 to 6
- cotangent: bfloat16 [1024, 768], P('expert', 'tensor'), may hold values from -6 to 6
- attn_gain: bfloat16 [768], replicated, may hold values from 0.5 to 1.5
- qkv_weight: bfloat16 [3, 768, 768], P(None, None, 'tensor'), may hold values from -0.21875 to 0.21875
- out_weight: bfloat16 [768, 768], P('tensor'), may hold values from -0.875 to 0.875
- bias_table: float32 [32, 12], P(None, 'tensor'), may hold values from -6 to 6
- ffn_gain: bfloat16 [768], replicated, may hold values from 0.5 to 1.5
- router_weight: bfloat16 [768, 8], replicated, may hold values from -0.15625 to 0.15625
- expert_in: bfloat16 [8, 768, 3072], P('expert', None, 'tensor'), may hold values from -0.21875 to 0.21875
- expert_out: bfloat16 [8, 3072, 768], P('expert', 'tensor'), may hold values from -7 to 7
- routes: int32 [1024, 2], P('expert'), may hold values from 0 to 7, all different within a row; in each aligned block of 128 rows (0 to 127, 128 to 255, ...) at most 42 rows name the same one
- buckets: int32 [128], replicated, may hold values from 0 to 31, as said below
Outputs:
- mixed: bfloat16 [1024, 768], P('expert', 'tensor')
- tokens_grad: bfloat16 [1024, 768], P('expert', 'tensor')
- attn_gain_grad: float32 [768], replicated
- qkv_weight_grad: float32 [3, 768, 768], P(None, None, 'tensor')
- out_weight_grad: float32 [768, 768], P('tensor')
- bias_table_grad: float32 [32, 12], P(None, 'tensor')
- ffn_gain_grad: float32 [768], replicated
- router_weight_grad: float32 [768, 8], replicated
- expert_in_grad: float32 [8, 768, 3072], P('expert', None, 'tensor')
- expert_out_grad: float32 [8, 3072, 768], P('expert', 'tensor')
Inputs may be any that keep to these rules, and one draw needn't show every extreme that they name: `routes`: each row names 2 different experts. Among the rows of one sequence no expert is named more than 42 times, and in some sequences one expert is named exactly 42 times. `buckets`: never falls as the distance grows; 0 at distance 0 and 31 at the largest distance.
All inputs are finite; a program needn't handle non-finite values.
Results may differ from a plain program's by a relative error of at most 0.024.
Values may be sent and summed in bfloat16 or wider, within the bound.
A program may use at most 64 MiB of HBM per device.

v0:
```python
import jax
import jax.numpy as jnp
from jax import lax
from jax.sharding import PartitionSpec as P

PRECISE = lax.Precision.HIGHEST
EPSILON = 1e-06
ROOT_HALF = 0.7071067811865476
INV_ROOT_TAU = 0.3989422804014327


def gelu_slope(values):
    return (
        0.5 * (1.0 + lax.erf(values * ROOT_HALF))
        + values * jnp.exp(-0.5 * values * values) * INV_ROOT_TAU
    )


def diagonal_sums(grid):
    heads_here, length, _ = grid.shape
    flipped = grid[:, :, ::-1]
    padded = jnp.concatenate([flipped, jnp.zeros_like(flipped)], axis=2).reshape(heads_here, -1)
    window = lax.slice_in_dim(padded, length - 1, length - 1 + length * (2 * length - 1), axis=1)
    window = window.reshape(heads_here, length, 2 * length - 1)
    return jnp.sum(window[:, :, :length], axis=1)


def send_back(rows):
    return lax.all_to_all(rows, "expert", split_axis=0, concat_axis=0, tiled=True)


def pick_from(pick_table, rows_back):
    return jnp.einsum("tc,cd->td", pick_table, rows_back, preferred_element_type=jnp.float32)


def per_device(
    tokens,
    cotangent,
    attn_gain,
    qkv_weight,
    out_weight,
    bias_table,
    ffn_gain,
    router_weight,
    expert_in,
    expert_out,
    routes,
    buckets,
):
    n_expert = lax.axis_size("expert")
    tensor_index = lax.axis_index("tensor")
    share_width = tokens.shape[1]
    whole_tok, whole_cot = (
        lax.all_gather(tokens, "tensor", axis=1, tiled=True),
        lax.all_gather(cotangent, "tensor", axis=1, tiled=True),
    )
    inputs = whole_tok.astype(jnp.float32)
    grad_out = whole_cot.astype(jnp.float32)
    seq_len, width = inputs.shape
    r_first = lax.rsqrt(jnp.mean(inputs * inputs, axis=-1, keepdims=True) + EPSILON)
    normed = (inputs * r_first * attn_gain.astype(jnp.float32)).astype(jnp.bfloat16)
    projected = jnp.einsum(
        "td,cdf->ctf", normed, qkv_weight, preferred_element_type=jnp.float32
    ).astype(jnp.bfloat16)
    heads_here = bias_table.shape[1]
    head_size = qkv_weight.shape[2] // heads_here
    queries = projected[0].reshape(seq_len, heads_here, head_size)
    keys_here = projected[1].reshape(seq_len, heads_here, head_size)
    values_here = projected[2].reshape(seq_len, heads_here, head_size)
    position = jnp.arange(seq_len, dtype=jnp.int32)
    spacing = position[:, None] - position[None, :]
    causal = spacing >= 0
    bucket_hot = (
        buckets[:, None] == jnp.arange(bias_table.shape[0], dtype=jnp.int32)[None, :]
    ).astype(jnp.float32)
    bias_rows = jnp.einsum("bh,tb->ht", bias_table, bucket_hot, precision=PRECISE)
    full_bias = jnp.take(bias_rows, jnp.maximum(spacing, 0), axis=1)

    def scores_of(query_in, key_in):
        raw_scores = (
            jnp.einsum("qhd,khd->hqk", query_in, key_in, preferred_element_type=jnp.float32) * 0.125
            + full_bias
        )
        return jnp.where(causal[None], raw_scores, -1e30)

    scores = scores_of(queries, keys_here)
    row_max = jnp.max(scores, axis=-1, keepdims=True)
    row_total = jnp.sum(jnp.exp(scores - row_max), axis=-1, keepdims=True)
    weights = (jnp.exp(scores - row_max) / row_total).astype(jnp.bfloat16)
    context = jnp.einsum(
        "hqk,khd->qhd", weights, values_here, preferred_element_type=jnp.float32
    ).astype(jnp.bfloat16)
    context = context.reshape(seq_len, heads_here * head_size)
    attended = lax.psum(jnp.dot(context, out_weight, preferred_element_type=jnp.float32), "tensor")
    residual = inputs + attended
    r_second = lax.rsqrt(jnp.mean(residual * residual, axis=-1, keepdims=True) + EPSILON)
    ffn_in = (residual * r_second * ffn_gain.astype(jnp.float32)).astype(jnp.bfloat16)
    logits = jnp.dot(ffn_in, router_weight, preferred_element_type=jnp.float32)
    router_probs = jax.nn.softmax(logits, axis=-1)
    experts = router_weight.shape[1]
    top_count = routes.shape[1]
    expert_ids = jnp.arange(experts, dtype=jnp.int32)
    chosen = routes[:, :, None] == expert_ids[None, None, :]
    gate_values = jnp.sum(jnp.where(chosen, router_probs[:, None, :], 0.0), axis=-1)
    capacity = 4 * top_count * seq_len // (3 * experts)
    exp_here = expert_in.shape[0]
    paired = routes.reshape(-1)
    pair_hot = (paired[:, None] == expert_ids[None, :]).astype(jnp.int32)
    earlier = jnp.cumsum(pair_hot, axis=0) - pair_hot
    slots = jnp.sum(earlier * pair_hot, axis=-1)
    targets = paired * capacity + slots
    target_pairs = targets.reshape(seq_len, top_count)
    columns = jnp.arange(experts * capacity, dtype=jnp.int32)
    pick_rows = [
        (target_pairs[:, ordinal : ordinal + 1] == columns[None, :]).astype(jnp.bfloat16)
        for ordinal in range(top_count)
    ]
    pick_all = sum(pick_rows)
    send_rows = jnp.einsum(
        "tc,td->cd", pick_all, ffn_in, preferred_element_type=jnp.float32
    ).astype(jnp.bfloat16)
    send_rows = send_rows.reshape(n_expert, exp_here, capacity, width)
    received = lax.all_to_all(send_rows, "expert", split_axis=0, concat_axis=0, tiled=True)
    hidden = jnp.einsum("necd,edf->necf", received, expert_in, preferred_element_type=jnp.float32)
    active = jax.nn.gelu(hidden, approximate=False).astype(jnp.bfloat16)
    part_out = jnp.einsum(
        "necf,efd->necd", active, expert_out, preferred_element_type=jnp.float32
    ).astype(jnp.bfloat16)
    returned = send_back(part_out)
    returned, kept_rows, kept_hidden = (returned, received, hidden)
    returned_rows = returned.reshape(experts * capacity, -1)
    picked = [pick_from(pick_rows[ordinal], returned_rows) for ordinal in range(top_count)]
    expert_part = sum(
        [gate_values[:, ordinal : ordinal + 1] * picked[ordinal] for ordinal in range(top_count)]
    )
    residual_share = lax.dynamic_slice_in_dim(residual, tensor_index * share_width, share_width, 1)
    expert_share = lax.psum_scatter(
        expert_part.astype(jnp.bfloat16), "tensor", scatter_dimension=1, tiled=True
    ).astype(jnp.float32)
    mixed = (residual_share + expert_share).astype(jnp.bfloat16)
    grad_rows_in = jnp.einsum("tc,td->cd", pick_all, whole_cot, preferred_element_type=jnp.float32)
    slot_gate = (
        jnp.zeros((experts * capacity,), jnp.float32).at[targets].set(gate_values.reshape(-1))
    )
    grad_send = (
        (slot_gate[:, None] * grad_rows_in)
        .astype(jnp.bfloat16)
        .reshape(n_expert, exp_here, capacity, width)
    )
    grad_recv = lax.all_to_all(grad_send, "expert", split_axis=0, concat_axis=0, tiled=True)
    active_kept = jax.nn.gelu(kept_hidden, approximate=False).astype(jnp.bfloat16)
    expert_out_grad = jnp.einsum(
        "necf,necd->efd", active_kept, grad_recv, preferred_element_type=jnp.float32
    )
    grad_active = jnp.einsum(
        "necd,efd->necf", grad_recv, expert_out, preferred_element_type=jnp.float32
    )
    grad_hidden = (grad_active * gelu_slope(kept_hidden)).astype(jnp.bfloat16)
    expert_in_grad = jnp.einsum(
        "necd,necf->edf", kept_rows, grad_hidden, preferred_element_type=jnp.float32
    )
    grad_rows_out = jnp.einsum(
        "necf,edf->necd", grad_hidden, expert_in, preferred_element_type=jnp.float32
    ).astype(jnp.bfloat16)
    grad_back = send_back(grad_rows_out).reshape(experts * capacity, -1)
    grad_from_experts = pick_from(pick_all, grad_back)
    gate_terms = jnp.stack(
        [jnp.sum(picked[ordinal] * grad_out, axis=-1) for ordinal in range(top_count)], axis=-1
    )
    grad_ffn_experts, grad_gates = (
        lax.psum(grad_from_experts.astype(jnp.bfloat16), "tensor").astype(jnp.float32),
        lax.psum(gate_terms.astype(jnp.bfloat16), "tensor").astype(jnp.float32),
    )
    grad_probs = jnp.sum(jnp.where(chosen, grad_gates[:, :, None], 0.0), axis=1)
    grad_logits = (
        router_probs * (grad_probs - jnp.sum(router_probs * grad_probs, axis=-1, keepdims=True))
    ).astype(jnp.bfloat16)
    router_grad = jnp.einsum("td,te->de", ffn_in, grad_logits, preferred_element_type=jnp.float32)
    grad_ffn_in = grad_ffn_experts + jnp.einsum(
        "te,de->td", grad_logits, router_weight, preferred_element_type=jnp.float32
    )
    ffn_gain_grad = jnp.sum(grad_ffn_in * residual * r_second, axis=0)
    scaled_second = grad_ffn_in * ffn_gain.astype(jnp.float32)
    grad_residual = (
        grad_out
        + r_second * scaled_second
        - residual * r_second**3 * jnp.mean(scaled_second * residual, axis=-1, keepdims=True)
    )
    grad_attended = grad_residual.astype(jnp.bfloat16)
    out_grad = jnp.einsum("tf,td->fd", context, grad_attended, preferred_element_type=jnp.float32)
    grad_context = jnp.einsum(
        "td,fd->tf", grad_attended, out_weight, preferred_element_type=jnp.float32
    ).astype(jnp.bfloat16)
    grad_context = grad_context.reshape(seq_len, heads_here, head_size)
    scores = scores_of(queries, keys_here)
    soft = jnp.exp(scores - row_max) / row_total
    grad_values = jnp.einsum(
        "hqk,qhd->khd", soft.astype(jnp.bfloat16), grad_context, preferred_element_type=jnp.float32
    ).astype(jnp.bfloat16)
    grad_weights = jnp.einsum(
        "qhd,khd->hqk", grad_context, values_here, preferred_element_type=jnp.float32
    )
    grad_scores = (
        soft * (grad_weights - jnp.sum(soft * grad_weights, axis=-1, keepdims=True))
    ).astype(jnp.bfloat16)
    grad_queries = (
        jnp.einsum("hqk,khd->qhd", grad_scores, keys_here, preferred_element_type=jnp.float32)
        * 0.125
    ).astype(jnp.bfloat16)
    grad_keys = (
        jnp.einsum("hqk,qhd->khd", grad_scores, queries, preferred_element_type=jnp.float32) * 0.125
    ).astype(jnp.bfloat16)
    distance_grad = diagonal_sums(grad_scores.astype(jnp.float32))
    table_grad = jnp.einsum("tb,ht->bh", bucket_hot, distance_grad, precision=PRECISE)
    grad_projected = jnp.stack(
        [
            grad_queries.reshape(seq_len, -1),
            grad_keys.reshape(seq_len, -1),
            grad_values.reshape(seq_len, -1),
        ]
    )
    qkv_grad = jnp.einsum("td,ctf->cdf", normed, grad_projected, preferred_element_type=jnp.float32)
    grad_normed_part = jnp.einsum(
        "ctf,cdf->td", grad_projected, qkv_weight, preferred_element_type=jnp.float32
    )
    grad_normed = lax.psum(grad_normed_part.astype(jnp.bfloat16), "tensor").astype(jnp.float32)
    attn_gain_grad = jnp.sum(grad_normed * inputs * r_first, axis=0)
    scaled_first = grad_normed * attn_gain.astype(jnp.float32)
    grad_inputs = (
        grad_residual
        + r_first * scaled_first
        - inputs * r_first**3 * jnp.mean(scaled_first * inputs, axis=-1, keepdims=True)
    )
    tokens_grad = lax.dynamic_slice_in_dim(
        grad_inputs, tensor_index * share_width, share_width, 1
    ).astype(jnp.bfloat16)
    summed = lax.psum(
        (attn_gain_grad, qkv_grad, out_grad, table_grad, ffn_gain_grad, router_grad), "expert"
    )
    return (
        mixed,
        tokens_grad,
        summed[0],
        summed[1],
        summed[2],
        summed[3],
        summed[4],
        summed[5],
        expert_in_grad,
        expert_out_grad,
    )


def solution(mesh):
    placed = (
        P("expert", "tensor"),
        P("expert", "tensor"),
        P(),
        P(None, None, "tensor"),
        P("tensor", None),
        P(None, "tensor"),
        P(),
        P(),
        P("expert", None, "tensor"),
        P("expert", "tensor", None),
        P("expert", None),
        P(),
    )
    return jax.shard_map(
        per_device,
        mesh=mesh,
        in_specs=placed,
        out_specs=(
            P("expert", "tensor"),
            P("expert", "tensor"),
            P(),
            P(None, None, "tensor"),
            P("tensor", None),
            P(None, "tensor"),
            P(),
            P(),
            P("expert", None, "tensor"),
            P("expert", "tensor", None),
        ),
        check_vma=False,
    )
```

profile of v0, /device:TPU:14, one launch (start us, length us, event | category | flops | bytes accessed | tf_op | source)
XLA Modules:
  0.0 434.5 jit_solution(12523968347764725851)
XLA Ops:
  7.3 6.0 %all_gather.6 = bf16[128,768]{0,1:T(8,128)(2,1)S(1)} all-gather(bf16[128,192]{0,1:T(8,128)(2,1)} %param.12), channel_id=1, replica_groups=mesh['expert'=8,'tensor'=4] {'tensor'}, dimensions={1}, use_global_device_ids=true | all-gather | bytes 245760 | tf_op jit(solution)/shard_map/all_gather | solution.py:54
  15.7 54.4 %gather_fusion = f32[16384,3]{1,0:T(8,128)} fusion(f32[3,128]{0,1:T(8,128)S(1)} %copy.93, s32[16384]{0:T(1024)S(1)} %bitcast_clamp_fusion), kind=kCustom, calls=%fused_computation | custom fusion | bytes 458752 | tf_op jit(solution)/shard_map/jit(_take)/gather | solution.py:77
  70.2 6.6 %copy.95 = f32[128,128,3]{0,1,2:T(8,128)S(1)} copy(f32[128,128,3]{2,1,0:T(8,128)} %bitcast.172) | data formatting | bytes 393216 | tf_op jit(solution)/shard_map/jit(_take)/gather | solution.py:77
  78.0 1.0 fusion.92
  80.7 31.1 %all-reduce.8.cloned.1.call-done = f32[128,768]{1,0:T(8,128)} async-done(((f32[128,768]{1,0:T(8,128)}), f32[128,768]{1,0:T(8,128)}) %all-reduce.8.cloned.1.call-update) | async-done | bytes 393232 | tf_op jit(solution)/shard_map/psum | solution.py:94
  111.9 1.1 multiply_reduce_fusion.2
  113.7 1.2 convolution_convert_fusion.2
  114.8 1.2 reshape.224
  116.0 19.7 %all_to_all.20 = bf16[8,1,42,768]{3,2,1,0:T(8,128)(2,1)S(1)} all-to-all(bf16[8,1,42,768]{3,2,1,0:T(8,128)(2,1)S(1)} %bitcast.174), channel_id=1, replica_groups=mesh['expert'=8,'tensor'=4] {'expert'}, dimensions={0} | all-to-all | bytes 1032192 | tf_op jit(solution)/shard_map/all_to_all | solution.py:123
  135.7 4.0 fusion.9
  140.5 1.4 fusion.4
  142.0 6.5 %all-to-all-start.1 = ((bf16[8,1,42,768]{3,2,1,0:T(8,128)(2,1)}), bf16[8,1,42,768]{3,2,1,0:T(8,128)(2,1)}, u32[]{:S(2)}, u32[]{:S(2)}) async-start(bf16[8,1,42,768]{3,2,1,0:T(8,128)(2,1)} %fusion.4), calls=%async_computation.1 | async-start | bytes 1179648 | tf_op jit(solution)/shard_map/all_to_all | solution.py:29
  148.5 5.6 %all_gather.7 = bf16[128,768]{0,1:T(8,128)(2,1)S(1)} all-gather(bf16[128,192]{0,1:T(8,128)(2,1)S(1)} %copy-done.23), channel_id=1, replica_groups=mesh['expert'=8,'tensor'=4] {'tensor'}, dimensions={1}, use_global_device_ids=true | all-gather | bytes 245760 | tf_op jit(solution)/shard_map/all_gather | solution.py:55
  155.3 5.1 %all-to-all-done.1 = bf16[8,1,42,768]{3,2,1,0:T(8,128)(2,1)} async-done(((bf16[8,1,42,768]{3,2,1,0:T(8,128)(2,1)}), bf16[8,1,42,768]{3,2,1,0:T(8,128)(2,1)}, u32[]{:S(2)}, u32[]{:S(2)}) %all-to-all-start.1) | async-done | bytes 516128 | tf_op jit(solution)/shard_map/all_to_all | solution.py:29
  160.4 1.2 reshape.229
  162.0 2.1 fusion.44
  164.1 5.8 %psum.72 = bf16[128,2]{0,1:T(2,128)(2,1)S(1)} all-reduce(bf16[128,2]{0,1:T(2,128)(2,1)S(1)} %pad_maximum_fusion.3), channel_id=1, replica_groups=mesh['expert'=8,'tensor'=4] {'tensor'}, use_global_device_ids=true, to_apply=%region_16.17 | all-reduce | flops 256 | bytes 1024 | tf_op jit(solution)/shard_map/psum | solution.py:172
  170.2 1.4 scatter_custom_fusion
  171.6 2.1 fusion.3
  173.7 1.2 reshape.231
  174.9 20.9 %all_to_all.21 = bf16[8,1,42,768]{3,2,1,0:T(8,128)(2,1)S(1)} all-to-all(bf16[8,1,42,768]{3,2,1,0:T(8,128)(2,1)S(1)} %bitcast.175), channel_id=1, replica_groups=mesh['expert'=8,'tensor'=4] {'expert'}, dimensions={0} | all-to-all | bytes 1032192 | tf_op jit(solution)/shard_map/all_to_all | solution.py:150
  195.8 2.3 fusion.6
  198.9 1.5 fusion.5
  200.4 6.5 %all-to-all-start.3 = ((bf16[8,1,42,768]{3,2,1,0:T(8,128)(2,1)}), bf16[8,1,42,768]{3,2,1,0:T(8,128)(2,1)}, u32[]{:S(2)}, u32[]{:S(2)}) async-start(bf16[8,1,42,768]{3,2,1,0:T(8,128)(2,1)} %fusion.5), calls=%async_computation.3 | async-start | bytes 1179648 | tf_op jit(solution)/shard_map/all_to_all | solution.py:29
  206.9 1.8 add_convert_fusion
  208.7 10.2 %all-to-all-done.3 = bf16[8,1,42,768]{3,2,1,0:T(8,128)(2,1)} async-done(((bf16[8,1,42,768]{3,2,1,0:T(8,128)(2,1)}), bf16[8,1,42,768]{3,2,1,0:T(8,128)(2,1)}, u32[]{:S(2)}, u32[]{:S(2)}) %all-to-all-start.3) | async-done | bytes 516128 | tf_op jit(solution)/shard_map/all_to_all | solution.py:29
  218.9 1.2 reshape.234
  220.1 1.0 convolution_convert_fusion.3
  221.2 1.7 copy.118
  223.2 30.4 %all-reduce.10.cloned.1.call-done = bf16[128,768]{1,0:T(8,128)(2,1)} async-done(((bf16[128,768]{1,0:T(8,128)(2,1)}), bf16[128,768]{1,0:T(8,128)(2,1)}) %all-reduce.10.cloned.1.call-update) | async-done | bytes 196624 | tf_op jit(solution)/shard_map/psum | solution.py:171
  253.6 1.3 multiply_reduce_fusion
  255.1 1.2 convolution_convert_fusion.6
  256.4 1.9 convolution_convert_fusion.4
  258.3 1.0 multiply_reduce_fusion.3
  260.0 1.0 fusion.31
  261.1 1.0 fusion.26
  262.2 2.5 convolution_bitcast_fusion.2
  264.7 1.0 fusion.59
  266.7 9.2 %reduce-scatter.4.cloned.1.call-done = bf16[192,128]{1,0:T(8,128)(2,1)} async-done(((bf16[768,128]{1,0:T(8,128)(2,1)}), bf16[192,128]{1,0:T(8,128)(2,1)}) %reduce-scatter.4.cloned.1.call-update) | async-done | bytes 49168
  275.8 0.9 copy.119
  277.6 3.4 convolution_bitcast_fusion.1
  281.0 2.2 convolution_bitcast_fusion
  284.9 24.8 %all-reduce.12.cloned.1.call-done = bf16[128,768]{1,0:T(8,128)(2,1)} async-done(((bf16[128,768]{1,0:T(8,128)(2,1)}), bf16[128,768]{1,0:T(8,128)(2,1)}) %all-reduce.12.cloned.1.call-update) | async-done | bytes 196624 | tf_op jit(solution)/shard_map/psum | solution.py:226
  309.7 1.1 fusion.43
  310.8 1.2 fusion.53
  312.7 32.7 %all-reduce.1 = (f32[768]{0:T(1024)}, f32[32,3]{0,1:T(4,128)}, f32[768]{0:T(1024)}, f32[768,8]{0,1:T(8,128)}) all-reduce(f32[768]{0:T(1024)S(1)} %get-tuple-element.62, f32[32,3]{0,1:T(4,128)S(1)} %fusion.70, f32[768]{0:T(1024)S(1)} %get-tuple-element.60, f32[768,8]{0,1:T(8,128)S(1)} %fusion.93), channel_id=1, replica_groups=mesh['expert'=8,'tensor'=4] {'expert'}, use_global_device_ids=true, to_apply=%region_24.25 | all-reduce | flops 7776 | bytes 62208 | tf_op jit(solution)/shard_map/psum | solution.py:237
  345.4 78.8 %all-reduce.14.cloned.1.call-done = (f32[3,768,192]{1,2,0:T(8,128)}, f32[192,768]{1,0:T(8,128)}) async-done(((f32[3,768,192]{1,2,0:T(8,128)}, f32[192,768]{1,0:T(8,128)}), (f32[3,768,192]{1,2,0:T(8,128)}, f32[192,768]{1,0:T(8,128)})) %all-reduce.14.cloned.1.call-update) | async-done | bytes 2359312 | tf_op jit(solution)/shard_map/psum | solution.py:237
  424.3 2.9 copy.127
  (153 shorter events, 15.9 us)
Async XLA Ops:
  7.2 128.5 %copy-start = (bf16[1,768,768]{2,1,0:T(8,128)(2,1)S(1)}, bf16[1,768,768]{2,1,0:T(8,128)(2,1)}, u32[]{:S(2)}) copy-start(bf16[1,768,768]{2,1,0:T(8,128)(2,1)} %param.20) | copy-start | bytes 3538948
  7.2 7.6 %copy-start.1 = (bf16[3,768,192]{1,2,0:T(8,128)(2,1)S(1)}, bf16[3,768,192]{1,2,0:T(8,128)(2,1)}, u32[]{:S(2)}) copy-start(bf16[3,768,192]{1,2,0:T(8,128)(2,1)} %param.15) | copy-start | bytes 2654212
  7.2 104.7 %all-reduce.8.cloned.1.call-start = ((), (), s32[]{:S(2)}) async-start(), calls=%async_computation.5 | async-start | bytes 786432 | tf_op jit(solution)/shard_map/psum | solution.py:94
  13.4 1.9 copy-start.34
  13.4 1.9 copy-start.35
  15.3 61.4 %copy-start.14 = (bf16[1,128,192]{1,2,0:T(8,128)(2,1)}, bf16[1,128,192]{1,2,0:T(8,128)(2,1)S(1)}, u32[]{:S(2)}) copy-start(bf16[1,128,192]{1,2,0:T(8,128)(2,1)S(1)} %get-tuple-element.79) | copy-start | bytes 147460
  15.3 61.4 %copy-start.16 = (bf16[1,128,192]{1,2,0:T(8,128)(2,1)}, bf16[1,128,192]{1,2,0:T(8,128)(2,1)S(1)}, u32[]{:S(2)}) copy-start(bf16[1,128,192]{1,2,0:T(8,128)(2,1)S(1)} %get-tuple-element.80) | copy-start | bytes 147460
  15.4 62.4 %copy-start.21 = (bf16[1,128,192]{1,2,0:T(8,128)(2,1)}, bf16[1,128,192]{1,2,0:T(8,128)(2,1)S(1)}, u32[]{:S(2)}) copy-start(bf16[1,128,192]{1,2,0:T(8,128)(2,1)S(1)} %get-tuple-element.81) | copy-start | bytes 147460
  76.7 1.3 copy-start.6
  77.0 2.0 copy-start.8
  77.0 2.0 copy-start.27
  77.8 2.8 copy-start.24
  77.8 2.8 copy-start.29
  78.0 35.0 %copy-start.17 = (bf16[3,64,128]{2,1,0:T(8,128)(2,1)}, bf16[3,64,128]{2,1,0:T(8,128)(2,1)S(1)}, u32[]{:S(2)}) copy-start(bf16[3,64,128]{2,1,0:T(8,128)(2,1)S(1)} %convolution_convert_fusion.5) | copy-start | bytes 147460
  113.5 2.5 copy-start.25
  135.7 4.0 copy-start.9
  135.7 4.8 %copy-start.32 = (bf16[1,768,768]{2,1,0:T(8,128)(2,1)S(1)}, bf16[1,768,768]{2,1,0:T(8,128)(2,1)}, u32[]{:S(2)}) copy-start(bf16[1,768,768]{2,1,0:T(8,128)(2,1)} %param.21) | copy-start | bytes 3538948
  139.7 0.8 copy-start.37
  142.0 6.5 %copy-start.23 = (bf16[128,192]{0,1:T(8,128)(2,1)S(1)}, bf16[128,192]{0,1:T(8,128)(2,1)}, u32[]{:S(2)}) copy-start(bf16[128,192]{0,1:T(8,128)(2,1)} %param.13) | copy-start | bytes 147460
  142.0 13.1 %copy-start.20 = (bf16[768,8]{0,1:T(8,128)(2,1)S(1)}, bf16[768,8]{0,1:T(8,128)(2,1)}, u32[]{:S(2)}) copy-start(bf16[768,8]{0,1:T(8,128)(2,1)} %param.19) | copy-start | bytes 36868
  142.0 18.4 %all-to-all-start.1 = ((bf16[8,1,42,768]{3,2,1,0:T(8,128)(2,1)}), bf16[8,1,42,768]{3,2,1,0:T(8,128)(2,1)}, u32[]{:S(2)}, u32[]{:S(2)}) async-start(bf16[8,1,42,768]{3,2,1,0:T(8,128)(2,1)} %fusion.4), calls=%async_computation.1 | async-start | bytes 1179648 | tf_op jit(solution)/shard_map/all_to_all | solution.py:29
  154.1 1.2 copy-start.5
  161.6 8.3 %copy-start.28 = (s32[128,2]{0,1:T(2,128)S(1)}, s32[128,2]{0,1:T(2,128)}, u32[]{:S(2)}) copy-start(s32[128,2]{0,1:T(2,128)} %param.22) | copy-start | bytes 3076
  162.0 2.2 copy-start.2
  174.9 20.9 %copy-start.33 = (bf16[1,768,768]{2,1,0:T(8,128)(2,1)S(1)}, bf16[1,768,768]{2,1,0:T(8,128)(2,1)}, u32[]{:S(2)}) copy-start(bf16[1,768,768]{2,1,0:T(8,128)(2,1)} %param.21) | copy-start | bytes 3538948
  195.8 2.3 copy-start.11
  198.1 0.8 copy-start.39
  200.4 6.5 %copy-start.3 = (f32[128,768]{1,0:T(8,128)S(1)}, f32[128,768]{1,0:T(8,128)}, u32[]{:S(2)}) copy-start(f32[128,768]{1,0:T(8,128)} %copy-done.2) | copy-start | bytes 1179652
  200.4 18.5 %all-to-all-start.3 = ((bf16[8,1,42,768]{3,2,1,0:T(8,128)(2,1)}), bf16[8,1,42,768]{3,2,1,0:T(8,128)(2,1)}, u32[]{:S(2)}, u32[]{:S(2)}) async-start(bf16[8,1,42,768]{3,2,1,0:T(8,128)(2,1)} %fusion.5), calls=%async_computation.3 | async-start | bytes 1179648 | tf_op jit(solution)/shard_map/all_to_all | solution.py:29
  206.9 46.7 %all-reduce.10.cloned.1.call-start = ((), (), s32[]{:S(2)}) async-start(), calls=%async_computation.6 | async-start | bytes 393216 | tf_op jit(solution)/shard_map/psum | solution.py:171
  208.7 44.9 %copy-start.26 = (f32[128]{0:T(128)S(1)}, f32[128]{0:T(128)}, u32[]{:S(2)}) copy-start(f32[128]{0:T(128)} %copy-done.25) | copy-start | bytes 1540
  220.1 34.8 %copy-start.31 = (f32[128]{0:T(128)S(1)}, f32[128]{0:T(128)}, u32[]{:S(2)}) copy-start(f32[128]{0:T(128)} %get-tuple-element.88) | copy-start | bytes 1540
  221.1 33.8 %copy-start.4 = (bf16[128,768]{1,0:T(8,128)(2,1)S(1)}, bf16[128,768]{1,0:T(8,128)(2,1)}, u32[]{:S(2)}) copy-start(bf16[128,768]{1,0:T(8,128)(2,1)} %copy.102) | copy-start | bytes 589828
  221.2 54.7 %reduce-scatter.4.cloned.1.call-start = ((), (), s32[]{:S(2)}) async-start(), calls=%async_computation.8 | async-start | bytes 245760
  223.0 86.7 %all-reduce.12.cloned.1.call-start = ((), (), s32[]{:S(2)}) async-start(), calls=%async_computation.7 | async-start | bytes 393216 | tf_op jit(solution)/shard_map/psum | solution.py:226
  255.1 3.2 copy-start.7
  255.1 3.2 copy-start.22
  258.3 2.7 copy-start.15
  258.3 2.8 copy-start.19
  262.2 2.5 copy-start.18
  264.6 159.6 %all-reduce.14.cloned.1.call-start = ((), (), s32[]{:S(2)}) async-start(), calls=%async_computation.9 | async-start | bytes 4718592 | tf_op jit(solution)/shard_map/psum | solution.py:237
  265.8 11.8 %copy-start.10 = (bf16[8,1,42,768]{3,2,1,0:T(8,128)(2,1)S(1)}, bf16[8,1,42,768]{3,2,1,0:T(8,128)(2,1)}, u32[]{:S(2)}) copy-start(bf16[8,1,42,768]{3,2,1,0:T(8,128)(2,1)} %copy-done.9) | copy-start | bytes 1548292
  277.6 3.4 copy-start.12
  277.6 3.4 copy-start.38
  283.7 0.9 copy-start.36
  284.1 26.7 %copy-start.30 = (f32[128]{0:T(128)S(1)}, f32[128]{0:T(128)}, u32[]{:S(2)}) copy-start(f32[128]{0:T(128)} %get-tuple-element.86) | copy-start | bytes 1540
  424.3 2.9 copy-start.13
Sparse Core Ops, SparseCore 0:
  79.1 32.7 all-reduce.7
  221.3 32.2 all-reduce.9
  256.0 19.7 reduce-scatter.3
  278.0 31.6 all-reduce.11
  314.1 110.0 all-reduce.13
where the time goes:
time: 438 us; the launch traced here: 434 us
  waiting for transfers between devices  190 us (43%)
  blocking collectives  90.5 us (21%)
  local copies, waits for them, and re-layouts  80.6 us (18%)
  matrix products  35.1 us (8%)
  between operations  14.4 us (3%)
  starting transfers between devices  13.3 us (3%)
  other arithmetic  10.7 us (2%)
    psum x1, waiting for transfers between devices, per_device(): lax.psum((attn_gain_grad, qkv_grad, out_grad, table_grad, ffn_gain_grad,...  78.8 us
    gather x2, local copies, waits for them, and re-layouts, per_device(): full_bias = jnp.take(bias_rows, jnp.maximum(spacing, 0), axis=1)  61 us
    psum x1, blocking collectives, per_device(): lax.psum((attn_gain_grad, qkv_grad, out_grad, table_grad, ffn_gain_grad,...  32.7 us
    psum x1, waiting for transfers between devices, per_device(): lax.psum(jnp.dot(context, out_weight, preferred_element_type=jnp.float32)...  31.1 us
    psum x1, waiting for transfers between devices, per_device(): lax.psum(grad_from_experts.astype(jnp.bfloat16), 'tensor')  30.4 us
    psum x1, waiting for transfers between devices, per_device(): lax.psum(grad_normed_part.astype(jnp.bfloat16), 'tensor')  24.8 us
    all_to_all x1, blocking collectives, per_device(): lax.all_to_all(grad_send, 'expert', split_axis=0, concat_axis=0, tiled=True)  20.9 us
    all_to_all x1, blocking collectives, per_device(): lax.all_to_all(send_rows, 'expert', split_axis=0, concat_axis=0, tiled=True)  19.7 us
  transfers between devices with their start and end apart: 7, of which 7 were waited for; matrix products, arithmetic and copies ran while one was open for 7% of the time, Pallas kernels for 0%

commit v1 on v0

v1 whole, which is shorter than its diff:
```python
import functools

import jax
import jax.numpy as jnp
from jax import lax
from jax.experimental import pallas as pl
from jax.experimental.pallas import tpu as pltpu
from jax.sharding import PartitionSpec as P

PRECISE = lax.Precision.HIGHEST
EPSILON = 1e-06
ROOT_HALF = 0.7071067811865476
INV_ROOT_TAU = 0.3989422804014327
F32 = jnp.float32
BF16 = jnp.bfloat16
MESH = pl.DeviceIdType.MESH


def exchange_kernel(plan, n_expert, n_tensor, *refs):
    count = len(plan)
    sources, results, sems = refs[:count], refs[count : 2 * count], refs[2 * count :]
    my_e, my_t = lax.axis_index("expert"), lax.axis_index("tensor")
    sizes = {"expert": n_expert, "tensor": n_tensor, "all": n_expert * n_tensor}

    def device_at(scope, step):
        if scope == "tensor":
            return my_e, lax.rem(my_t + step, n_tensor)
        if scope == "expert":
            return lax.rem(my_e + step, n_expert), my_t
        place = lax.rem(my_e * n_tensor + my_t + step, n_expert * n_tensor)
        return place // n_tensor, lax.rem(place, n_tensor)

    def slot_of(scope, e, t):
        return {"expert": (e,), "tensor": (t,), "all": (e, t)}[scope]

    def number_of(scope, e, t):
        return {"expert": e, "tensor": t, "all": e * n_tensor + t}[scope]

    scopes = []
    for scope, _ in plan:
        if scope not in scopes:
            scopes.append(scope)
    if "all" in scopes:
        scopes = ["all"]
    barrier = pltpu.get_barrier_semaphore()
    for scope in scopes:

        def greet(step, carry, scope=scope):
            pl.semaphore_signal(barrier, inc=1, device_id=device_at(scope, step), device_id_type=MESH)
            return carry

        lax.fori_loop(1, sizes[scope], greet, 0)
    pl.semaphore_wait(barrier, sum(sizes[scope] - 1 for scope in scopes))

    def copy_of(k, step, back):
        scope, kind = plan[k]
        e, t = device_at(scope, step)
        source = sources[k]
        if kind == "split":
            source = source.at[slot_of(scope, e, t)]
        if back:
            e2, t2 = device_at(scope, sizes[scope] - step)
            place, number = slot_of(scope, e2, t2), number_of(scope, e2, t2)
        else:
            place, number = slot_of(scope, my_e, my_t), number_of(scope, my_e, my_t)
        return pltpu.make_async_remote_copy(
            src_ref=source,
            dst_ref=results[k].at[place],
            send_sem=sems[3 * k].at[number_of(scope, e, t)],
            recv_sem=sems[3 * k + 1].at[number],
            device_id=(e, t),
            device_id_type=MESH,
        )

    own = []
    for k, (scope, kind) in enumerate(plan):

        def start(step, carry, k=k):
            copy_of(k, step, False).start()
            return carry

        lax.fori_loop(1, sizes[scope], start, 0)
        mine = slot_of(scope, my_e, my_t)
        source = sources[k].at[mine] if kind == "split" else sources[k]
        copy = pltpu.make_async_copy(source, results[k].at[mine], sems[3 * k + 2])
        copy.start()
        own.append(copy)
    for k, (scope, kind) in enumerate(plan):

        def finish(step, carry, k=k):
            copy_of(k, step, False).wait_send()
            copy_of(k, step, True).wait_recv()
            return carry

        lax.fori_loop(1, sizes[scope], finish, 0)
        own[k].wait()


def exchange(number, *moves):
    n_expert, n_tensor = lax.axis_size("expert"), lax.axis_size("tensor")
    lead = {"expert": (n_expert,), "tensor": (n_tensor,), "all": (n_expert, n_tensor)}
    plan = tuple((scope, kind) for scope, kind, _ in moves)
    arrays = [array for _, _, array in moves]
    shapes, scratch = [], []
    for scope, kind, array in moves:
        shape = array.shape if kind == "split" else lead[scope] + array.shape
        shapes.append(jax.ShapeDtypeStruct(shape, array.dtype))
        amount = 1
        for size in lead[scope]:
            amount *= size
        scratch += [
            pltpu.SemaphoreType.DMA((amount,)),
            pltpu.SemaphoreType.DMA((amount,)),
            pltpu.SemaphoreType.DMA,
        ]
    return pl.pallas_call(
        functools.partial(exchange_kernel, plan, n_expert, n_tensor),
        out_shape=tuple(shapes),
        in_specs=[pl.BlockSpec(memory_space=pl.ANY)] * len(arrays),
        out_specs=tuple([pl.BlockSpec(memory_space=pl.ANY)] * len(arrays)),
        scratch_shapes=scratch,
        compiler_params=pltpu.CompilerParams(collective_id=number, has_side_effects=True),
    )(*arrays)


def gelu_slope(values):
    return (
        0.5 * (1.0 + lax.erf(values * ROOT_HALF))
        + values * jnp.exp(-0.5 * values * values) * INV_ROOT_TAU
    )


def diagonal_sums(grid):
    heads_here, length, _ = grid.shape
    flipped = grid[:, :, ::-1]
    padded = jnp.concatenate([flipped, jnp.zeros_like(flipped)], axis=2).reshape(heads_here, -1)
    window = lax.slice_in_dim(padded, length - 1, length - 1 + length * (2 * length - 1), axis=1)
    window = window.reshape(heads_here, length, 2 * length - 1)
    return jnp.sum(window[:, :, :length], axis=1)


def spread_diagonals(rows):
    heads_here, length = rows.shape
    period = jnp.concatenate(
        [rows[:, :1], jnp.zeros((heads_here, length), F32), rows[:, :0:-1]], axis=1
    )
    flat = jnp.tile(period, (1, length))[:, : length * (2 * length - 1)]
    return flat.reshape(heads_here, length, 2 * length - 1)[:, :, :length]


def two_parts(values):
    high = lax.reduce_precision(values, 8, 7)
    return high.astype(BF16), (values - high).astype(BF16)


def dot(a, b, dims):
    return lax.dot_general(a, b, (dims, ((), ())), preferred_element_type=F32)


def per_device(
    tokens,
    cotangent,
    attn_gain,
    qkv_weight,
    out_weight,
    bias_table,
    ffn_gain,
    router_weight,
    expert_in,
    expert_out,
    routes,
    buckets,
):
    n_expert, n_tensor = lax.axis_size("expert"), lax.axis_size("tensor")
    tensor_index = lax.axis_index("tensor")
    seq_len, share = tokens.shape
    width = share * n_tensor
    heads_here = bias_table.shape[1]
    local = qkv_weight.shape[2]
    head_size = local // heads_here
    experts = router_weight.shape[1]
    top_count = routes.shape[1]
    capacity = 4 * top_count * seq_len // (3 * experts)
    rows_each = -(-(capacity + 2) // 16) * 16
    all_rows = experts * rows_each

    (both,) = exchange(0, ("tensor", "whole", jnp.concatenate([tokens, cotangent], axis=1)))
    both = both.transpose(1, 0, 2)
    inputs = both[:, :, :share].reshape(seq_len, width).astype(F32)
    whole_cot = both[:, :, share:].reshape(seq_len, width)
    grad_out = whole_cot.astype(F32)

    expert_ids = jnp.arange(experts, dtype=jnp.int32)
    chosen = routes[:, :, None] == expert_ids[None, None, :]
    paired = routes.reshape(-1)
    pair_hot = (paired[:, None] == expert_ids[None, :]).astype(F32)
    order = jnp.arange(seq_len * top_count, dtype=jnp.int32)
    before = (order[:, None] > order[None, :]).astype(BF16)
    earlier = dot(before, pair_hot.astype(BF16), ((1,), (0,)))
    slots = jnp.sum(earlier * pair_hot, axis=-1).astype(jnp.int32)
    target_pairs = (paired * rows_each + slots).reshape(seq_len, top_count)
    back_pairs = (paired * (n_tensor * rows_each) + slots).reshape(seq_len, top_count)
    columns = jnp.arange(all_rows, dtype=jnp.int32)
    picks = [target_pairs[:, k : k + 1] == columns[None, :] for k in range(top_count)]
    pick_all = sum([pick.astype(BF16) for pick in picks])
    cot_rows = dot(pick_all, whole_cot, ((0,), (0,))).astype(BF16)

    r_first = lax.rsqrt(jnp.mean(inputs * inputs, axis=-1, keepdims=True) + EPSILON)
    normed = (inputs * r_first * attn_gain.astype(F32)).astype(BF16)
    projected = jnp.einsum("td,cdf->ctf", normed, qkv_weight, preferred_element_type=F32).astype(BF16)
    queries = projected[0].reshape(seq_len, heads_here, head_size)
    keys_here = projected[1].reshape(seq_len, heads_here, head_size)
    values_here = projected[2].reshape(seq_len, heads_here, head_size)
    position = jnp.arange(seq_len, dtype=jnp.int32)
    causal = position[:, None] >= position[None, :]
    bucket_hot = (
        buckets[:, None] == jnp.arange(bias_table.shape[0], dtype=jnp.int32)[None, :]
    ).astype(F32)
    bias_rows = jnp.einsum("bh,tb->ht", bias_table, bucket_hot, precision=PRECISE)
    full_bias = spread_diagonals(bias_rows)
    raw_scores = (
        jnp.einsum("qhd,khd->hqk", queries, keys_here, preferred_element_type=F32) * 0.125 + full_bias
    )
    scores = jnp.where(causal[None], raw_scores, -1e30)
    row_max = jnp.max(scores, axis=-1, keepdims=True)
    powers = jnp.exp(scores - row_max)
    soft = powers / jnp.sum(powers, axis=-1, keepdims=True)
    weights = soft.astype(BF16)
    context = jnp.einsum("hqk,khd->qhd", weights, values_here, preferred_element_type=F32)
    context = context.astype(BF16).reshape(seq_len, local)

    whole_context, whole_out, cot_recv = exchange(
        1,
        ("tensor", "whole", context),
        ("tensor", "whole", out_weight),
        ("expert", "split", cot_rows.reshape(n_expert, rows_each, width)),
    )
    attended = dot(
        whole_context.transpose(1, 0, 2).reshape(seq_len, width),
        whole_out.reshape(width, width),
        ((1,), (0,)),
    )
    residual = inputs + attended
    r_second = lax.rsqrt(jnp.mean(residual * residual, axis=-1, keepdims=True) + EPSILON)
    ffn_in = (residual * r_second * ffn_gain.astype(F32)).astype(BF16)
    router_probs = jax.nn.softmax(dot(ffn_in, router_weight, ((1,), (0,))), axis=-1)
    gate_values = jnp.sum(jnp.where(chosen, router_probs[:, None, :], 0.0), axis=-1)
    slot_gate = sum(
        [
            jnp.sum(jnp.where(picks[k], gate_values[:, k : k + 1], 0.0), axis=0)
            for k in range(top_count)
        ]
    ).reshape(n_expert, rows_each)
    line = jnp.arange(rows_each, dtype=jnp.int32)

    def add_lines(body, values):
        extra = body.ndim - 3
        high, low = [
            jnp.pad(part, ((0, 0), (0, body.shape[-1] - rows_each))).reshape(
                (n_expert,) + (1,) * (extra + 1) + (body.shape[-1],)
            )
            for part in two_parts(values)
        ]
        at = line[:, None]
        return jnp.where(at == capacity, high, jnp.where(at == capacity + 1, low, body))

    def read_lines(body):
        return (
            body[..., capacity, :rows_each].astype(F32)
            + body[..., capacity + 1, :rows_each].astype(F32)
        )

    send_rows = dot(pick_all, ffn_in, ((0,), (0,))).astype(BF16).reshape(n_expert, rows_each, width)
    (received,) = exchange(2, ("expert", "split", add_lines(send_rows, slot_gate)))
    row_gate = read_lines(received).reshape(all_rows, 1)
    kept_rows = jnp.where((line < capacity)[None, :, None], received, 0).reshape(all_rows, width)
    w_in, w_out = expert_in[0], expert_out[0]
    hidden = dot(kept_rows, w_in, ((1,), (0,)))
    active = jax.nn.gelu(hidden, approximate=False).astype(BF16)
    part_out = dot(active, w_out, ((1,), (0,))).astype(BF16)
    cot_here = cot_recv.reshape(all_rows, width).astype(F32)
    grad_part = (row_gate * cot_here).astype(BF16)
    grad_active = dot(grad_part, w_out, ((1,), (1,)))
    grad_hidden = (grad_active * gelu_slope(hidden)).astype(BF16)
    grad_rows = dot(grad_hidden, w_in, ((1,), (1,))).astype(BF16)
    row_dots = jnp.sum(part_out.astype(F32) * cot_here, axis=-1).reshape(n_expert, rows_each)
    expert_out_grad = dot(active, grad_part, ((0,), (0,)))[None]
    expert_in_grad = dot(kept_rows, grad_hidden, ((0,), (0,)))[None]

    back = jnp.concatenate(
        [
            part_out.reshape(n_expert, rows_each, n_tensor, share),
            grad_rows.reshape(n_expert, rows_each, n_tensor, share),
        ],
        axis=-1,
    ).transpose(0, 2, 1, 3)
    (returned,) = exchange(3, ("all", "split", add_lines(back, row_dots)))
    slot_dots = jnp.sum(read_lines(returned), axis=1).reshape(1, all_rows)
    grad_gates = jnp.stack(
        [jnp.sum(jnp.where(picks[k], slot_dots, 0.0), axis=-1) for k in range(top_count)], axis=-1
    )
    places = jnp.arange(n_tensor * all_rows, dtype=jnp.int32)
    group_start = places - (places // rows_each % n_tensor) * rows_each
    back_pick = jnp.concatenate(
        [back_pairs[:, k : k + 1] == group_start[None, :] for k in range(top_count)], axis=0
    ).astype(BF16)
    picked = dot(back_pick, returned.reshape(n_tensor * all_rows, 2 * share), ((1,), (0,)))
    picked = picked.reshape(top_count, seq_len, 2 * share)
    expert_share = sum([gate_values[:, k : k + 1] * picked[k, :, :share] for k in range(top_count)])
    residual_share = lax.dynamic_slice_in_dim(residual, tensor_index * share, share, 1)
    mixed = (residual_share + expert_share).astype(BF16)

    grad_ffn_share = jnp.sum(picked[:, :, share:], axis=0).astype(BF16)
    (grad_ffn_experts,) = exchange(4, ("tensor", "whole", grad_ffn_share))
    grad_ffn_experts = grad_ffn_experts.transpose(1, 0, 2).reshape(seq_len, width).astype(F32)
    grad_probs = jnp.sum(jnp.where(chosen, grad_gates[:, :, None], 0.0), axis=1)
    grad_logits = (
        router_probs * (grad_probs - jnp.sum(router_probs * grad_probs, axis=-1, keepdims=True))
    ).astype(BF16)
    router_grad = dot(grad_logits, ffn_in, ((0,), (0,)))
    grad_ffn_in = grad_ffn_experts + dot(grad_logits, router_weight, ((1,), (1,)))
    ffn_gain_grad = jnp.sum(grad_ffn_in * residual * r_second, axis=0)
    scaled_second = grad_ffn_in * ffn_gain.astype(F32)
    grad_residual = (
        grad_out
        + r_second * scaled_second
        - residual * r_second**3 * jnp.mean(scaled_second * residual, axis=-1, keepdims=True)
    )
    grad_attended = grad_residual.astype(BF16)
    grad_context = dot(grad_attended, out_weight, ((1,), (1,))).astype(BF16)
    grad_context = grad_context.reshape(seq_len, heads_here, head_size)
    grad_values = jnp.einsum("hqk,qhd->khd", weights, grad_context, preferred_element_type=F32)
    grad_weights = jnp.einsum("qhd,khd->hqk", grad_context, values_here, preferred_element_type=F32)
    grad_scores = (
        soft * (grad_weights - jnp.sum(soft * grad_weights, axis=-1, keepdims=True))
    ).astype(BF16)
    grad_queries = jnp.einsum("hqk,khd->qhd", grad_scores, keys_here, preferred_element_type=F32) * 0.125
    grad_keys = jnp.einsum("hqk,qhd->khd", grad_scores, queries, preferred_element_type=F32) * 0.125
    distance_grad = diagonal_sums(grad_scores.astype(F32))
    table_grad = jnp.einsum("tb,ht->bh", bucket_hot, distance_grad, precision=PRECISE)
    grad_projected = jnp.concatenate(
        [part.astype(BF16).reshape(seq_len, local) for part in (grad_queries, grad_keys, grad_values)],
        axis=1,
    )
    qkv_flat = qkv_weight.transpose(1, 0, 2).reshape(width, 3 * local)
    grad_normed_part = dot(grad_projected, qkv_flat, ((1,), (1,)))
    qkv_grad = dot(normed, grad_projected, ((0,), (0,)))
    out_grad = dot(grad_attended, context, ((0,), (0,)))
    attn_part = jnp.sum(grad_normed_part * inputs * r_first, axis=0)
    row_part = jnp.sum(grad_normed_part * attn_gain.astype(F32) * inputs, axis=-1, keepdims=True)
    row_high, row_low = two_parts(row_part)
    shares = grad_normed_part.astype(BF16).reshape(seq_len, n_tensor, share).transpose(1, 0, 2)
    pad = (-share - 2) % 128
    tail = jnp.concatenate([row_high, row_low, jnp.zeros((seq_len, pad), BF16)], axis=1)
    shares = jnp.concatenate(
        [shares, jnp.broadcast_to(tail[None], (n_tensor,) + tail.shape)], axis=2
    )
    table_line = jnp.pad(table_grad.reshape(1, -1), ((0, 0), (0, width - table_grad.size)))
    pack = jnp.concatenate([attn_part[None], ffn_gain_grad[None], table_line, router_grad], axis=0)
    pack = jnp.pad(pack, ((0, -pack.shape[0] % 8), (0, 0)))
    grads = jnp.concatenate([qkv_grad, out_grad], axis=1)
    block = width // n_expert
    if block % 16 == 0:
        blocks, packs, normed_parts = exchange(
            5,
            ("expert", "split", grads.astype(BF16).reshape(n_expert, block, -1)),
            ("expert", "whole", pack),
            ("tensor", "split", shares),
        )
        block_sum = jnp.sum(blocks.astype(F32), axis=0).astype(BF16)
    else:
        packs, normed_parts = exchange(
            5, ("expert", "whole", pack), ("tensor", "split", shares)
        )
    pack = jnp.sum(packs, axis=0)
    attn_rows = jnp.pad(pack[:1], ((0, 7), (0, 0)))
    if block % 16 == 0:
        grads, attn_rows = exchange(
            6, ("expert", "whole", block_sum), ("tensor", "whole", attn_rows)
        )
        grads = grads.reshape(width, -1).astype(F32)
    else:
        (attn_rows,) = exchange(6, ("tensor", "whole", attn_rows))
        grads = lax.psum(grads, "expert")
    attn_gain_grad = jnp.sum(attn_rows[:, 0], axis=0)
    normed_sum = jnp.sum(normed_parts.astype(F32), axis=0)
    row_mean = (normed_sum[:, share : share + 1] + normed_sum[:, share + 1 : share + 2]) / width

    def own_share(values):
        return lax.dynamic_slice_in_dim(values, tensor_index * share, share, values.ndim - 1)

    own_inputs = tokens.astype(F32)
    tokens_grad = (
        own_share(grad_residual)
        + r_first * (normed_sum[:, :share] * own_share(attn_gain.astype(F32)))
        - own_inputs * r_first**3 * row_mean
    ).astype(BF16)
    qkv_out = grads[:, : 3 * local].reshape(width, 3, local).transpose(1, 0, 2)
    return (
        mixed,
        tokens_grad,
        attn_gain_grad,
        qkv_out,
        grads[:, 3 * local :].T,
        pack[2, : table_grad.size].reshape(table_grad.shape),
        pack[1],
        pack[3 : 3 + experts].T,
        expert_in_grad,
        expert_out_grad,
    )


def solution(mesh):
    placed = (
        P("expert", "tensor"),
        P("expert", "tensor"),
        P(),
        P(None, None, "tensor"),
        P("tensor", None),
        P(None, "tensor"),
        P(),
        P(),
        P("expert", None, "tensor"),
        P("expert", "tensor", None),
        P("expert", None),
        P(),
    )
    return jax.shard_map(
        per_device,
        mesh=mesh,
        in_specs=placed,
        out_specs=(
            P("expert", "tensor"),
            P("expert", "tensor"),
            P(),
            P(None, None, "tensor"),
            P("tensor", None),
            P(None, "tensor"),
            P(),
            P(),
            P("expert", None, "tensor"),
            P("expert", "tensor", None),
        ),
        check_vma=False,
    )
```

time: 438 us -> 261 us (0.60)
  waiting for transfers between devices: 190 us -> 0 us
  Pallas kernels: 0 us -> 151 us
  blocking collectives: 90.5 us -> 0 us
  local copies, waits for them, and re-layouts: 80.6 us -> 40.2 us
  other arithmetic: 10.7 us -> 33.6 us
  starting transfers between devices: 13.3 us -> 0 us
  between operations: 14.4 us -> 1.56 us
    psum x4 -> x0, waiting for transfers between devices: 165 us -> none  [the longest x1 78.8 us: per_device(): lax.psum((attn_gain_grad, qkv_grad, out_grad, table_grad, ffn_gain_grad,...]
    pallas_call x0 -> x7, Pallas kernels: none -> 151 us  [exchange(): pl.pallas_call(functools.partial(exchange_kernel, plan, n_expert, n_tenso...]
    gather x2 -> x0, local copies, waits for them, and re-layouts: 61 us -> none  [per_device(): full_bias = jnp.take(bias_rows, jnp.maximum(spacing, 0), axis=1)]
    all_to_all x2 -> x0, blocking collectives: 40.5 us -> none  [the longest x1 20.9 us: per_device(): lax.all_to_all(grad_send, 'expert', split_axis=0, concat_axis=0, tiled=True)]
    psum x2 -> x0, blocking collectives: 38.5 us -> none  [the longest x1 32.7 us: per_device(): lax.psum((attn_gain_grad, qkv_grad, out_grad, table_grad, ffn_gain_grad,...]
    all_to_all x2 -> x0, waiting for transfers between devices: 15.3 us -> none  [send_back(): lax.all_to_all(rows, 'expert', split_axis=0, concat_axis=0, tiled=True)]
    all_to_all x2 -> x0, starting transfers between devices: 13 us -> none  [send_back(): lax.all_to_all(rows, 'expert', split_axis=0, concat_axis=0, tiled=True)]
    all_gather x2 -> x0, blocking collectives: 11.5 us -> none  [the longest x1 5.95 us: per_device(): lax.all_gather(tokens, 'tensor', axis=1, tiled=True)]
  transfers between devices with their start and end apart: 7 -> 0, of which waited for: 7 -> 0; matrix products, arithmetic and copies ran while one was open for 7% -> 0% of each run, Pallas kernels for 0% -> 0%
where the time goes in v1:
time: 261 us; the launch traced here: 260 us
  Pallas kernels  151 us (58%)
  local copies, waits for them, and re-layouts  40.2 us (15%)
  matrix products  34 us (13%)
  other arithmetic  33.6 us (13%)
    pallas_call x7, Pallas kernels, exchange(): pl.pallas_call(functools.partial(exchange_kernel, plan, n_expert, n_tenso...  151 us
    dot_general x18, matrix products, dot(): return lax.dot_general(a, b, (dims, ((), ())), preferred_element_type=F32)  28.5 us
    unnamed x99, local copies, waits for them, and re-layouts  7.41 us

profile of v1, /device:TPU:14, one launch (start us, length us, event | category | flops | bytes accessed | tf_op | source)
XLA Modules:
  0.0 260.1 jit_solution(3655876030284700325)
XLA Ops:
  4.9 6.0 %shard_map.195 = bf16[4,128,384]{2,1,0:T(8,128)(2,1)} custom-call(bf16[128,384]{1,0:T(8,128)(2,1)} %pad_maximum_fusion.3.refs_0_), custom_call_target="tpu_custom_call" | custom-call | tf_op jit(solution)/shard_map/pallas_call | solution.py:116
  10.9 1.9 fusion.83
  13.7 1.2 copy.178
  20.1 1.3 convolution_convert_fusion.2
  21.3 19.4 %shard_map.196 = (bf16[4,128,192]{2,1,0:T(8,128)(2,1)}, bf16[4,192,768]{2,1,0:T(8,128)(2,1)}, bf16[8,48,768]{2,1,0:T(8,128)(2,1)}) custom-call(bf16[128,192]{1,0:T(8,128)(2,1)} %copy.176.refs_0_, bf16[192,768]{1,0:T(8,128)(2,1)} %refs_1_.1, bf16[8,48,768]{2,1,0:T(8,128)(2,1)} %bitcast.186), custom_call_target="tpu_custom_call" | custom-call | tf_op jit(solution)/shard_map/pallas_call | solution.py:116
  40.8 1.8 multiply_reduce_fusion.5
  43.3 1.3 convolution_convert_fusion.1
  45.1 2.0 select_select_fusion.refs_0_
  47.2 17.9 %shard_map.197 = bf16[8,48,768]{2,1,0:T(8,128)(2,1)} custom-call(bf16[8,48,768]{2,1,0:T(8,128)(2,1)} %select_select_fusion.refs_0_), custom_call_target="tpu_custom_call" | custom-call | tf_op jit(solution)/shard_map/pallas_call | solution.py:116
  65.5 1.5 fusion.82
  67.1 1.3 fusion.12
  68.6 4.0 %fusion.5 = (bf16[384,768]{1,0:T(8,128)(2,1)}, f32[384,768]{1,0:T(8,128)S(1)}) fusion(bf16[384,768]{1,0:T(8,128)(2,1)S(1)} %bitcast.183, bf16[1,768,768]{2,1,0:T(8,128)(2,1)S(1)} %copy-done.39), kind=kOutput, calls=%fused_computation.19 | convolution fusion | flops 472154112 | bytes 3538944 | tf_op jit(solution)/shard_map/dot_general | solution.py:157
  74.2 1.5 convolution_convert_fusion.3
  75.7 2.9 %reshape.288 = bf16[8,48,4,192]{3,2,1,0:T(4,128)(2,1)} reshape(bf16[384,768]{1,0:T(8,128)(2,1)} %convolution_convert_fusion.3) | data formatting | bytes 1179648 | tf_op jit(solution)/shard_map/reshape | solution.py:293
  78.6 2.1 copy.181
  80.8 2.9 %fusion.14 = (bf16[384,768]{1,0:T(8,128)(2,1)}, f32[384]{0:T(512)S(1)}, bf16[384,768]{1,0:T(8,128)(2,1)}) fusion(bf16[8,48,768]{2,1,0:T(8,128)(2,1)} %get-tuple-element.20, f32[384]{0:T(512)S(1)} %add.146, bf16[384,768]{1,0:T(8,128)(2,1)} %get-tuple-element.123, bf16[1,768,768]{2,1,0:T(8,128)(2,1)S(1)} %copy-done), kind=kOutput, calls=%fused_computation.34 | convolution fusion | flops 455048832 | bytes 3542016 | tf_op jit(solution)/shard_map/dot_general | solution.py:157
  83.8 2.9 %reshape.287 = bf16[8,48,4,192]{3,2,1,0:T(4,128)(2,1)} reshape(bf16[384,768]{1,0:T(8,128)(2,1)} %get-tuple-element.125) | data formatting | bytes 1179648 | tf_op jit(solution)/shard_map/reshape | solution.py:292
  86.7 2.1 copy.180
  89.0 3.0 %fusion.11.refs_0_ = bf16[8,4,48,384]{3,2,1,0:T(8,128)(2,1)} fusion(bf16[8,48,4,192]{3,1,2,0:T(8,128)(2,1)} %copy.181, bf16[8,48,4,192]{3,1,2,0:T(8,128)(2,1)} %copy.180, pred[48]{0:T(512)(128)(4,1)S(1)} %get-tuple-element.131, pred[48]{0:T(512)(128)(4,1)S(1)} %get-tuple-element.132, bf16[8,384]{1,0:T(8,128)(2,1)S(1)} %pad.30, bf16[8,384]{1,0:T(8,128)(2,1)S(1)} %pad.29), kind=kLoop, calls=%fused_computation.26 | loop fusion | flops 3538944 | bytes 2371680 | tf_op jit(solution)/shard_map/jit(_where)/select_n | solution.py:265
  92.0 32.0 %shard_map.198 = bf16[8,4,48,384]{3,2,1,0:T(8,128)(2,1)} custom-call(bf16[8,4,48,384]{3,2,1,0:T(8,128)(2,1)} %fusion.11.refs_0_), custom_call_target="tpu_custom_call" | custom-call | tf_op jit(solution)/shard_map/pallas_call | solution.py:116
  124.0 2.7 %fusion.87 = f32[2,128,384]{2,1,0:T(8,128)} fusion(pred[2,128,1536]{2,1,0:T(32,128)(4,1)} %bitcast.210, bf16[1536,384,1]{1,0,2:T(8,128)(2,1)} %bitcast.194), kind=kOutput, calls=%fused_computation.212 | convolution fusion | flops 301989888 | bytes 1966080 | tf_op jit(solution)/shard_map/dot_general | solution.py:157
  128.6 1.7 slice_reduce_fusion.refs_0_
  130.3 5.4 %shard_map.199 = bf16[4,128,192]{2,1,0:T(8,128)(2,1)} custom-call(bf16[128,192]{1,0:T(8,128)(2,1)} %slice_reduce_fusion.refs_0_), custom_call_target="tpu_custom_call" | custom-call | tf_op jit(solution)/shard_map/pallas_call | solution.py:116
  135.7 1.8 convert_bitcast_fusion
  137.5 2.0 copy.183
  139.5 1.9 copy.184
  142.7 2.0 multiply_reduce_fusion.2
  146.1 2.0 convert_bitcast_fusion.2
  148.1 1.8 copy.189
  149.8 1.2 convolution_convert_fusion.5
  151.0 1.2 convolution_convert_fusion.8
  152.2 1.9 convolution_convert_fusion.6
  154.1 1.2 multiply_reduce_fusion.6
  157.5 1.7 multiply_reduce_fusion.1
  160.2 1.3 convolution_convert_fusion
  161.5 1.2 pad_maximum_fusion.refs_0_
  167.1 39.9 %shard_map.200 = (bf16[8,96,768]{2,1,0:T(8,128)(2,1)}, f32[8,16,768]{2,1,0:T(8,128)}, bf16[4,128,256]{2,1,0:T(8,128)(2,1)}) custom-call(bf16[8,96,768]{2,1,0:T(8,128)(2,1)} %pad_maximum_fusion.refs_0_, f32[16,768]{1,0:T(8,128)} %pad.32.refs_1_, bf16[4,128,256]{2,1,0:T(8,128)(2,1)} %pad_maximum_fusion.1.refs_2_), custom_call_target="tpu_custom_call" | custom-call | tf_op jit(solution)/shard_map/pallas_call | solution.py:116
  209.3 2.1 reduce_sum.253.refs_0_
  212.1 30.2 %shard_map.201 = (bf16[8,96,768]{2,1,0:T(8,128)(2,1)}, f32[4,8,768]{2,1,0:T(8,128)}) custom-call(bf16[96,768]{1,0:T(8,128)(2,1)} %reduce_sum.253.refs_0_, f32[8,768]{1,0:T(8,128)} %get-tuple-element.96.refs_1_), custom_call_target="tpu_custom_call" | custom-call | tf_op jit(solution)/shard_map/pallas_call | solution.py:116
  242.3 1.5 slice_reduce_fusion.2
  243.8 1.4 bitcast_convert_fusion
  245.3 1.4 slice.155
  246.7 2.8 %copy.199 = f32[768,576]{0,1:T(8,128)} copy(f32[768,576]{1,0:T(8,128)} %slice.155) | data formatting | bytes 3538944 | tf_op jit(solution)/shard_map/slice | solution.py:398
  249.4 1.1 slice.156
  250.6 2.3 copy.211
  254.3 1.3 slice_reduce_fusion.3
  255.7 2.2 convolution_bitcast_fusion.1
  257.9 2.2 convolution_bitcast_fusion
  (199 shorter events, 30.0 us)
Async XLA Ops:
  0.6 71.9 %copy-start = (bf16[1,768,768]{2,1,0:T(8,128)(2,1)S(1)}, bf16[1,768,768]{2,1,0:T(8,128)(2,1)}, u32[]{:S(2)}) copy-start(bf16[1,768,768]{2,1,0:T(8,128)(2,1)} %param.21) | copy-start | bytes 3538948
  0.7 3.3 %copy-start.24 = (bf16[128,192]{0,1:T(8,128)(2,1)S(1)}, bf16[128,192]{0,1:T(8,128)(2,1)}, u32[]{:S(2)}) copy-start(bf16[128,192]{0,1:T(8,128)(2,1)} %param.13) | copy-start | bytes 147460
  0.7 3.4 %copy-start.25 = (bf16[128,192]{0,1:T(8,128)(2,1)S(1)}, bf16[128,192]{0,1:T(8,128)(2,1)}, u32[]{:S(2)}) copy-start(bf16[128,192]{0,1:T(8,128)(2,1)} %param.12) | copy-start | bytes 147460
  4.1 6.8 %copy-start.13 = (bf16[128,192]{1,0:T(8,128)(2,1)}, bf16[128,192]{1,0:T(8,128)(2,1)S(1)}, u32[]{:S(2)}) copy-start(bf16[128,192]{1,0:T(8,128)(2,1)S(1)} %copy.167) | copy-start | bytes 147460
  12.8 2.1 copy-start.33
  12.8 2.1 copy-start.2
  12.8 2.8 %copy-start.1 = (bf16[3,768,192]{1,2,0:T(8,128)(2,1)S(1)}, bf16[3,768,192]{1,2,0:T(8,128)(2,1)}, u32[]{:S(2)}) copy-start(bf16[3,768,192]{1,2,0:T(8,128)(2,1)} %param.15) | copy-start | bytes 2654212
  15.1 1.1 copy-start.40
  15.1 1.1 copy-start.41
  15.6 0.8 copy-start.30
  16.1 1.8 copy-start.15
  16.2 1.8 copy-start.17
  17.8 2.1 copy-start.6
  18.2 3.1 %copy-start.8 = (f32[3,128,128]{1,2,0:T(8,128)}, f32[3,128,128]{1,2,0:T(8,128)S(1)}, u32[]{:S(2)}) copy-start(f32[3,128,128]{1,2,0:T(8,128)S(1)} %fusion.30) | copy-start | bytes 589828
  19.0 21.8 %copy-start.27 = (f32[3,128]{1,0:T(4,128)}, f32[3,128]{1,0:T(4,128)S(1)}, u32[]{:S(2)}) copy-start(f32[3,128]{1,0:T(4,128)S(1)} %get-tuple-element.117) | copy-start | bytes 4612
  40.8 1.9 copy-start.35
  42.6 1.9 copy-start.23
  42.6 2.2 copy-start.26
  43.2 99.6 %copy-start.29 = (f32[128]{0:T(128)}, f32[128]{0:T(128)S(1)}, u32[]{:S(2)}) copy-start(f32[128]{0:T(128)S(1)} %get-tuple-element.116) | copy-start | bytes 1540
  65.5 2.9 %copy-start.3 = (bf16[8,48,768]{2,1,0:T(8,128)(2,1)S(1)}, bf16[8,48,768]{2,1,0:T(8,128)(2,1)}, u32[]{:S(2)}) copy-start(bf16[8,48,768]{2,1,0:T(8,128)(2,1)} %shard_map.197) | copy-start | bytes 1769476
  67.1 1.5 copy-start.39
  68.5 4.0 %copy-start.4 = (bf16[8,48,768]{2,1,0:T(8,128)(2,1)}, bf16[8,48,768]{2,1,0:T(8,128)(2,1)S(1)}, u32[]{:S(2)}) copy-start(bf16[8,48,768]{2,1,0:T(8,128)(2,1)S(1)} %broadcast_select_fusion) | copy-start | bytes 1769476
  73.4 0.8 copy-start.10
  148.1 4.2 %copy-start.28 = (f32[3,128]{1,0:T(4,128)S(1)}, f32[3,128]{1,0:T(4,128)}, u32[]{:S(2)}) copy-start(f32[3,128]{1,0:T(4,128)} %copy-done.27) | copy-start | bytes 4612
  154.1 3.2 %copy-start.16 = (bf16[1,128,192]{1,2,0:T(8,128)(2,1)S(1)}, bf16[1,128,192]{1,2,0:T(8,128)(2,1)}, u32[]{:S(2)}) copy-start(bf16[1,128,192]{1,2,0:T(8,128)(2,1)} %copy-done.15) | copy-start | bytes 147460
  154.1 3.3 %copy-start.22 = (bf16[3,64,128]{2,1,0:T(8,128)(2,1)S(1)}, bf16[3,64,128]{2,1,0:T(8,128)(2,1)}, u32[]{:S(2)}) copy-start(bf16[3,64,128]{2,1,0:T(8,128)(2,1)} %convolution_convert_fusion.6) | copy-start | bytes 147460
  154.1 3.3 %copy-start.31 = (f32[128]{0:T(128)S(1)}, f32[128]{0:T(128)}, u32[]{:S(2)}) copy-start(f32[128]{0:T(128)} %copy-done.30) | copy-start | bytes 1540
  157.2 1.9 copy-start.18
  157.4 1.7 copy-start.19
  163.3 1.0 copy-start.42
  163.3 2.1 copy-start.38
  163.6 2.3 copy-start.7
  166.3 42.0 %copy-start.34 = (bf16[768]{0:T(1024)(128)(2,1)S(1)}, bf16[768]{0:T(1024)(128)(2,1)}, u32[]{:S(2)}) copy-start(bf16[768]{0:T(1024)(128)(2,1)} %param.14) | copy-start | bytes 4612
  166.3 42.1 %copy-start.14 = (bf16[128,192]{1,0:T(8,128)(2,1)S(1)}, bf16[128,192]{1,0:T(8,128)(2,1)}, u32[]{:S(2)}) copy-start(bf16[128,192]{1,0:T(8,128)(2,1)} %copy-done.13) | copy-start | bytes 147460
  166.3 42.1 %copy-start.32 = (f32[128]{0:T(128)S(1)}, f32[128]{0:T(128)}, u32[]{:S(2)}) copy-start(f32[128]{0:T(128)} %copy-done.30) | copy-start | bytes 1540
  166.3 42.1 %copy-start.37 = (f32[128]{0:T(128)S(1)}, f32[128]{0:T(128)}, u32[]{:S(2)}) copy-start(f32[128]{0:T(128)} %get-tuple-element.111) | copy-start | bytes 1540
  207.0 4.4 %copy-start.20 = (f32[8,16,768]{2,1,0:T(8,128)S(1)}, f32[8,16,768]{2,1,0:T(8,128)}, u32[]{:S(2)}) copy-start(f32[8,16,768]{2,1,0:T(8,128)} %get-tuple-element.23) | copy-start | bytes 1179652
  208.1 3.3 %copy-start.36 = (pred[8]{0:T(512)(128)(4,1)S(1)}, pred[8]{0:T(512)(128)(4,1)}, u32[]{:S(2)}) copy-start(pred[8]{0:T(512)(128)(4,1)} %constant.132.clone.1) | copy-start | bytes 28
  211.4 32.4 %copy-start.21 = (f32[16,768]{1,0:T(8,128)}, f32[16,768]{1,0:T(8,128)S(1)}, u32[]{:S(2)}) copy-start(f32[16,768]{1,0:T(8,128)S(1)} %reduce_sum.254) | copy-start | bytes 147460
  250.6 5.1 %copy-start.5 = (bf16[8,48,768]{2,1,0:T(8,128)(2,1)S(1)}, bf16[8,48,768]{2,1,0:T(8,128)(2,1)}, u32[]{:S(2)}) copy-start(bf16[8,48,768]{2,1,0:T(8,128)(2,1)} %copy-done.4) | copy-start | bytes 1769476
  250.6 5.1 %copy-start.11 = (bf16[384,768]{1,0:T(8,128)(2,1)S(1)}, bf16[384,768]{1,0:T(8,128)(2,1)}, u32[]{:S(2)}) copy-start(bf16[384,768]{1,0:T(8,128)(2,1)} %copy-done.10) | copy-start | bytes 1769476
  255.7 2.2 copy-start.9
  255.7 2.2 copy-start.12

commit v2 on v1

--- a/solution.py
+++ b/solution.py
@@ -72,6 +72,37 @@
             device_id_type=MESH,
         )
 
+    def relay_of(k, step, stage):
+        scope = plan[k][0]
+        half = sizes[scope] // 2
+        me = my_e if scope == "expert" else my_t
+        high, low = me // 2, lax.rem(me, 2)
+        other = 1 - low
+        after = lax.rem(high + step, half)
+        before = lax.rem(high + half - step, half)
+        target, origin, number = {
+            "out": (after * 2 + low, me, after * 2 + low),
+            "in": (after * 2 + low, before * 2 + low, 0),
+            "pair": (high * 2 + other, me, high * 2 + other),
+            "on": (high * 2 + other, before * 2 + low, before * 2 + other),
+            "over": (high * 2 + other, before * 2 + other, 0),
+        }[stage]
+        return pltpu.make_async_remote_copy(
+            src_ref=results[k].at[origin] if stage == "on" else sources[k],
+            dst_ref=results[k].at[origin],
+            send_sem=sems[3 * k].at[number],
+            recv_sem=sems[3 * k + 1].at[origin],
+            device_id=(target, my_t) if scope == "expert" else (my_e, target),
+            device_id_type=MESH,
+        )
+
+    def steps(k, stage, act, first=1):
+        def one(step, carry):
+            getattr(relay_of(k, step, stage), act)()
+            return carry
+
+        lax.fori_loop(first, sizes[plan[k][0]] // 2, one, 0)
+
     own = []
     for k, (scope, kind) in enumerate(plan):
 
@@ -79,20 +110,39 @@
             copy_of(k, step, False).start()
             return carry
 
-        lax.fori_loop(1, sizes[scope], start, 0)
+        if kind == "relay":
+            steps(k, "out", "start")
+            relay_of(k, 0, "pair").start()
+        else:
+            lax.fori_loop(1, sizes[scope], start, 0)
         mine = slot_of(scope, my_e, my_t)
         source = sources[k].at[mine] if kind == "split" else sources[k]
         copy = pltpu.make_async_copy(source, results[k].at[mine], sems[3 * k + 2])
         copy.start()
         own.append(copy)
     for k, (scope, kind) in enumerate(plan):
+        if kind == "relay":
+
+            def pass_on(step, carry, k=k):
+                relay_of(k, step, "in").wait_recv()
+                relay_of(k, step, "on").start()
+                return carry
+
+            lax.fori_loop(1, sizes[scope] // 2, pass_on, 0)
+    for k, (scope, kind) in enumerate(plan):
 
         def finish(step, carry, k=k):
             copy_of(k, step, False).wait_send()
             copy_of(k, step, True).wait_recv()
             return carry
 
-        lax.fori_loop(1, sizes[scope], finish, 0)
+        if kind == "relay":
+            steps(k, "out", "wait_send")
+            relay_of(k, 0, "pair").wait_send()
+            steps(k, "on", "wait_send")
+            steps(k, "over", "wait_recv", 0)
+        else:
+            lax.fori_loop(1, sizes[scope], finish, 0)
         own[k].wait()
 
 
@@ -123,11 +173,68 @@
     )(*arrays)
 
 
-def gelu_slope(values):
-    return (
-        0.5 * (1.0 + lax.erf(values * ROOT_HALF))
-        + values * jnp.exp(-0.5 * values * values) * INV_ROOT_TAU
-    )
+def expert_kernel(capacity, rows_ref, cot_ref, in_ref, out_ref, back_ref, in_grad, out_grad, kept, gated, part, grad_rows):
+    n_expert, rows_each, width = rows_ref.shape
+    n_tensor, share = back_ref.shape[1], back_ref.shape[3] // 2
+    all_rows = n_expert * rows_each
+    line = lax.broadcasted_iota(jnp.int32, (rows_each, 1), 0)
+    diagonal = line == lax.broadcasted_iota(jnp.int32, (rows_each, 128), 1)
+
+    def fill(e, carry):
+        rows = rows_ref[e].astype(F32)
+        kept[e] = jnp.where(line < capacity, rows, 0.0).astype(BF16)
+        gates = rows[capacity : capacity + 1, :128] + rows[capacity + 1 : capacity + 2, :128]
+        gate = jnp.sum(jnp.where(diagonal, gates, 0.0), axis=1, keepdims=True)
+        gated[e] = (gate * cot_ref[e].astype(F32)).astype(BF16)
+        return carry
+
+    lax.fori_loop(0, n_expert, fill, 0)
+    inputs = kept[...].reshape(all_rows, width)
+    hidden = dot(inputs, in_ref[...], ((1,), (0,)))
+    normal = 0.5 * (1.0 + lax.erf(hidden * ROOT_HALF))
+    active = (hidden * normal).astype(BF16)
+    slope = normal + hidden * jnp.exp(-0.5 * hidden * hidden) * INV_ROOT_TAU
+    part[...] = dot(active, out_ref[...], ((1,), (0,))).astype(BF16).reshape(part.shape)
+    grads = gated[...].reshape(all_rows, width)
+    grad_hidden = (dot(grads, out_ref[...], ((1,), (1,))) * slope).astype(BF16)
+    grad_rows[...] = dot(grad_hidden, in_ref[...], ((1,), (1,))).astype(BF16).reshape(part.shape)
+
+    def send(e, carry):
+        forward, backward = part[e], grad_rows[e]
+        dots = jnp.sum(forward.astype(F32) * cot_ref[e].astype(F32), axis=1, keepdims=True)
+        row = jnp.sum(jnp.where(diagonal, dots, 0.0), axis=0, keepdims=True)
+        high = row.astype(BF16).astype(F32)
+        blank = jnp.zeros((1, 2 * share - 128), F32)
+        high, low = [jnp.concatenate([x, blank], axis=1) for x in (high, row - high)]
+        for g in range(n_tensor):
+            span = slice(g * share, (g + 1) * share)
+            body = jnp.concatenate([forward[:, span], backward[:, span]], axis=1).astype(F32)
+            body = jnp.where(line == capacity, high, jnp.where(line == capacity + 1, low, body))
+            back_ref[e, g] = body.astype(BF16)
+        return carry
+
+    lax.fori_loop(0, n_expert, send, 0)
+    out_grad[...] = dot(active, grads, ((0,), (0,)))
+    in_grad[...] = dot(inputs, grad_hidden, ((0,), (0,)))
+
+
+def run_expert(rows, cot_rows, w_in, w_out, capacity, n_tensor):
+    n_expert, rows_each, width = rows.shape
+    share = width // n_tensor
+    inner = w_in.shape[1]
+    vmem = pl.BlockSpec(memory_space=pltpu.VMEM)
+    return pl.pallas_call(
+        functools.partial(expert_kernel, capacity),
+        out_shape=(
+            jax.ShapeDtypeStruct((n_expert, n_tensor, rows_each, 2 * share), BF16),
+            jax.ShapeDtypeStruct((width, inner), F32),
+            jax.ShapeDtypeStruct((inner, width), F32),
+        ),
+        in_specs=[vmem] * 4,
+        out_specs=(vmem,) * 3,
+        scratch_shapes=[pltpu.VMEM((n_expert, rows_each, width), BF16)] * 4,
+        compiler_params=pltpu.CompilerParams(vmem_limit_bytes=48 << 20),
+    )(rows, cot_rows, w_in, w_out)
 
 
 def diagonal_sums(grid):
@@ -184,7 +291,13 @@
     rows_each = -(-(capacity + 2) // 16) * 16
     all_rows = experts * rows_each
 
-    (both,) = exchange(0, ("tensor", "whole", jnp.concatenate([tokens, cotangent], axis=1)))
+    block = width // n_expert
+    gathers = block % 16 == 0
+    both, *share_rows = exchange(
+        0,
+        ("tensor", "whole", jnp.concatenate([tokens, cotangent], axis=1)),
+        *([("expert", "relay", tokens)] if gathers else []),
+    )
     both = both.transpose(1, 0, 2)
     inputs = both[:, :, :share].reshape(seq_len, width).astype(F32)
     whole_cot = both[:, :, share:].reshape(seq_len, width)
@@ -206,7 +319,8 @@
     cot_rows = dot(pick_all, whole_cot, ((0,), (0,))).astype(BF16)
 
     r_first = lax.rsqrt(jnp.mean(inputs * inputs, axis=-1, keepdims=True) + EPSILON)
-    normed = (inputs * r_first * attn_gain.astype(F32)).astype(BF16)
+    gain = attn_gain.astype(F32)
+    normed = (inputs * r_first * gain).astype(BF16)
     projected = jnp.einsum("td,cdf->ctf", normed, qkv_weight, preferred_element_type=F32).astype(BF16)
     queries = projected[0].reshape(seq_len, heads_here, head_size)
     keys_here = projected[1].reshape(seq_len, heads_here, head_size)
@@ -231,8 +345,8 @@
 
     whole_context, whole_out, cot_recv = exchange(
         1,
-        ("tensor", "whole", context),
-        ("tensor", "whole", out_weight),
+        ("tensor", "relay", context),
+        ("tensor", "relay", out_weight),
         ("expert", "split", cot_rows.reshape(n_expert, rows_each, width)),
     )
     attended = dot(
@@ -271,30 +385,16 @@
         )
 
     send_rows = dot(pick_all, ffn_in, ((0,), (0,))).astype(BF16).reshape(n_expert, rows_each, width)
-    (received,) = exchange(2, ("expert", "split", add_lines(send_rows, slot_gate)))
-    row_gate = read_lines(received).reshape(all_rows, 1)
-    kept_rows = jnp.where((line < capacity)[None, :, None], received, 0).reshape(all_rows, width)
-    w_in, w_out = expert_in[0], expert_out[0]
-    hidden = dot(kept_rows, w_in, ((1,), (0,)))
-    active = jax.nn.gelu(hidden, approximate=False).astype(BF16)
-    part_out = dot(active, w_out, ((1,), (0,))).astype(BF16)
-    cot_here = cot_recv.reshape(all_rows, width).astype(F32)
-    grad_part = (row_gate * cot_here).astype(BF16)
-    grad_active = dot(grad_part, w_out, ((1,), (1,)))
-    grad_hidden = (grad_active * gelu_slope(hidden)).astype(BF16)
-    grad_rows = dot(grad_hidden, w_in, ((1,), (1,))).astype(BF16)
-    row_dots = jnp.sum(part_out.astype(F32) * cot_here, axis=-1).reshape(n_expert, rows_each)
-    expert_out_grad = dot(active, grad_part, ((0,), (0,)))[None]
-    expert_in_grad = dot(kept_rows, grad_hidden, ((0,), (0,)))[None]
-
-    back = jnp.concatenate(
-        [
-            part_out.reshape(n_expert, rows_each, n_tensor, share),
-            grad_rows.reshape(n_expert, rows_each, n_tensor, share),
-        ],
-        axis=-1,
-    ).transpose(0, 2, 1, 3)
-    (returned,) = exchange(3, ("all", "split", add_lines(back, row_dots)))
+    received, *all_tokens = exchange(
+        2,
+        ("expert", "split", add_lines(send_rows, slot_gate)),
+        *[("tensor", "relay", rows.reshape(n_expert * seq_len, share)) for rows in share_rows],
+    )
+    back, expert_in_grad, expert_out_grad = run_expert(
+        received, cot_recv, expert_in[0], expert_out[0], capacity, n_tensor
+    )
+    expert_in_grad, expert_out_grad = expert_in_grad[None], expert_out_grad[None]
+    (returned,) = exchange(3, ("all", "split", back))
     slot_dots = jnp.sum(read_lines(returned), axis=1).reshape(1, all_rows)
     grad_gates = jnp.stack(
         [jnp.sum(jnp.where(picks[k], slot_dots, 0.0), axis=-1) for k in range(top_count)], axis=-1
@@ -344,7 +444,6 @@
     )
     qkv_flat = qkv_weight.transpose(1, 0, 2).reshape(width, 3 * local)
     grad_normed_part = dot(grad_projected, qkv_flat, ((1,), (1,)))
-    qkv_grad = dot(normed, grad_projected, ((0,), (0,)))
     out_grad = dot(grad_attended, context, ((0,), (0,)))
     attn_part = jnp.sum(grad_normed_part * inputs * r_first, axis=0)
     row_part = jnp.sum(grad_normed_part * attn_gain.astype(F32) * inputs, axis=-1, keepdims=True)
@@ -357,31 +456,38 @@
     )
     table_line = jnp.pad(table_grad.reshape(1, -1), ((0, 0), (0, width - table_grad.size)))
     pack = jnp.concatenate([attn_part[None], ffn_gain_grad[None], table_line, router_grad], axis=0)
-    pack = jnp.pad(pack, ((0, -pack.shape[0] % 8), (0, 0)))
-    grads = jnp.concatenate([qkv_grad, out_grad], axis=1)
-    block = width // n_expert
-    if block % 16 == 0:
-        blocks, packs, normed_parts = exchange(
-            5,
-            ("expert", "split", grads.astype(BF16).reshape(n_expert, block, -1)),
-            ("expert", "whole", pack),
-            ("tensor", "split", shares),
+    pack = jnp.pad(pack, ((0, -pack.shape[0] % 16), (0, 0)))
+    moves = [("expert", "relay", pack.astype(BF16)), ("tensor", "split", shares)]
+    if gathers:
+        pieces = out_grad.astype(BF16).reshape(n_expert, block, local)
+        all_projected, packs, normed_parts, pieces = exchange(
+            5, ("expert", "relay", grad_projected), *moves, ("expert", "split", pieces)
         )
-        block_sum = jnp.sum(blocks.astype(F32), axis=0).astype(BF16)
+        piece = jnp.sum(pieces.astype(F32), axis=0).astype(BF16)
     else:
-        packs, normed_parts = exchange(
-            5, ("expert", "whole", pack), ("tensor", "split", shares)
+        packs, normed_parts = exchange(5, *moves)
+    pack = jnp.sum(packs.astype(F32), axis=0)
+    attn_rows = jnp.pad(pack[:1], ((0, 7), (0, 0)))
+    if gathers:
+        pieces, attn_rows = exchange(
+            6, ("expert", "relay", piece), ("tensor", "whole", attn_rows)
         )
-    pack = jnp.sum(packs, axis=0)
-    attn_rows = jnp.pad(pack[:1], ((0, 7), (0, 0)))
-    if block % 16 == 0:
-        grads, attn_rows = exchange(
-            6, ("expert", "whole", block_sum), ("tensor", "whole", attn_rows)
-        )
-        grads = grads.reshape(width, -1).astype(F32)
+        out_grad = pieces.reshape(width, local).astype(F32)
+        all_tokens = all_tokens[0].transpose(1, 0, 2).reshape(n_expert * seq_len, width).astype(F32)
+        all_r = lax.rsqrt(jnp.mean(all_tokens * all_tokens, axis=-1, keepdims=True) + EPSILON)
+        all_normed = (all_tokens * all_r * gain).astype(BF16)
+        all_projected = all_projected.reshape(n_expert * seq_len, 3 * local)
     else:
         (attn_rows,) = exchange(6, ("tensor", "whole", attn_rows))
-        grads = lax.psum(grads, "expert")
+        all_normed, all_projected = normed, grad_projected
+    qkv_grad = jnp.stack(
+        [
+            dot(all_normed, all_projected[:, c * local : (c + 1) * local], ((0,), (0,)))
+            for c in range(3)
+        ]
+    )
+    if not gathers:
+        out_grad, qkv_grad = lax.psum((out_grad, qkv_grad), "expert")
     attn_gain_grad = jnp.sum(attn_rows[:, 0], axis=0)
     normed_sum = jnp.sum(normed_parts.astype(F32), axis=0)
     row_mean = (normed_sum[:, share : share + 1] + normed_sum[:, share + 1 : share + 2]) / width
@@ -395,13 +501,12 @@
         + r_first * (normed_sum[:, :share] * own_share(attn_gain.astype(F32)))
         - own_inputs * r_first**3 * row_mean
     ).astype(BF16)
-    qkv_out = grads[:, : 3 * local].reshape(width, 3, local).transpose(1, 0, 2)
     return (
         mixed,
         tokens_grad,
         attn_gain_grad,
-        qkv_out,
-        grads[:, 3 * local :].T,
+        qkv_grad,
+        out_grad.T,
         pack[2, : table_grad.size].reshape(table_grad.shape),
         pack[1],
         pack[3 : 3 + experts].T,

time: 261 us -> 235 us (0.900); the launches traced: 260 us -> 230 us
  matrix products: 34 us -> 18.8 us
  Pallas kernels: 151 us -> 143 us
  local copies, waits for them, and re-layouts: 40.2 us -> 32.8 us
    dot_general x18 -> x14, matrix products: 28.5 us -> 13.4 us  [dot(): return lax.dot_general(a, b, (dims, ((), ())), preferred_element_type=F32)]
    pallas_call x7, Pallas kernels: 151 us -> 136 us  [exchange(): pl.pallas_call(functools.partial(exchange_kernel, plan, n_expert, n_tenso...]
    reshape x5 -> x3, local copies, waits for them, and re-layouts: 10.2 us -> 0.34 us  [per_device(): part.astype(BF16).reshape(seq_len, local)]
    pallas_call x0 -> x1, Pallas kernels: none -> 7.07 us  [run_expert(): pl.pallas_call(functools.partial(expert_kernel, capacity), out_shape=(jax...]
    convert_element_type x0 -> x2, local copies, waits for them, and re-layouts: none -> 6.19 us  [the longest x1 5.27 us: per_device(): all_tokens[0].transpose(1, 0, 2).reshape(n_expert * seq_len, width)]
    slice x3 -> x0, local copies, waits for them, and re-layouts: 5.3 us -> none  [the longest x2 4.15 us: per_device(): qkv_out = grads[:, :3 * local].reshape(width, 3, local).transpose(1, 0, 2)]
    select_n x2 -> x1, other arithmetic: 5.04 us -> 0.94 us  [add_lines(): jnp.where(at == capacity, high, jnp.where(at == capacity + 1, low, body))]
    dot_general x2 -> x0, local copies, waits for them, and re-layouts: 2.84 us -> none  [dot(): return lax.dot_general(a, b, (dims, ((), ())), preferred_element_type=F32)]
where the time goes in v2:
time: 235 us; the launch traced here: 230 us
  Pallas kernels  143 us (61%)
  other arithmetic  34 us (14%)
  local copies, waits for them, and re-layouts  32.8 us (14%)
  matrix products  18.8 us (8%)
    pallas_call x7, Pallas kernels, exchange(): pl.pallas_call(functools.partial(exchange_kernel, plan, n_expert, n_tenso...  136 us
    dot_general x14, matrix products, dot(): return lax.dot_general(a, b, (dims, ((), ())), preferred_element_type=F32)  13.4 us
    unnamed x82, local copies, waits for them, and re-layouts  9.03 us
    pallas_call x1, Pallas kernels, run_expert(): pl.pallas_call(functools.partial(expert_kernel, capacity), out_shape=(jax...  7.07 us
    convert_element_type x1, local copies, waits for them, and re-layouts, per_device(): all_tokens[0].transpose(1, 0, 2).reshape(n_expert * seq_len, width)  5.27 us

profile of v2, /device:TPU:14, one launch (start us, length us, event | category | flops | bytes accessed | tf_op | source)
XLA Modules:
  0.0 230.3 jit_solution(3378439146334065014)
XLA Ops:
  0.7 1.2 copy-done
  2.5 1.3 dynamic_slice.11
  3.8 0.9 convolution_bitcast_fusion.4
  6.4 0.9 copy.172.refs_1_
  7.3 0.9 copy.173
  13.3 13.9 %shard_map.195 = (bf16[4,128,384]{2,1,0:T(8,128)(2,1)}, bf16[8,128,192]{2,1,0:T(8,128)(2,1)}) custom-call(bf16[128,384]{1,0:T(8,128)(2,1)} %pad_maximum_fusion.3.refs_0_, bf16[128,192]{1,0:T(8,128)(2,1)} %copy-done.12), custom_call_target="tpu_custom_call" | custom-call | tf_op jit(solution)/shard_map/pallas_call | solution.py:166
  27.2 1.1 multiply_reduce_fusion
  28.9 1.2 fusion.59
  30.2 0.8 copy.186
  31.1 1.2 convolution_convert_fusion.1
  35.2 17.6 %shard_map.196 = (bf16[4,128,192]{2,1,0:T(8,128)(2,1)}, bf16[4,192,768]{2,1,0:T(8,128)(2,1)}, bf16[8,48,768]{2,1,0:T(8,128)(2,1)}) custom-call(bf16[128,192]{1,0:T(8,128)(2,1)} %copy.182.refs_0_, bf16[192,768]{1,0:T(8,128)(2,1)} %refs_1_.2, bf16[8,48,768]{2,1,0:T(8,128)(2,1)} %bitcast.154), custom_call_target="tpu_custom_call" | custom-call | tf_op jit(solution)/shard_map/pallas_call | solution.py:166
  52.8 1.8 multiply_reduce_fusion.5
  56.9 0.9 select_select_fusion.refs_0_
  57.8 21.8 %shard_map.197 = (bf16[8,48,768]{2,1,0:T(8,128)(2,1)}, bf16[4,1024,192]{2,1,0:T(8,128)(2,1)}) custom-call(bf16[8,48,768]{2,1,0:T(8,128)(2,1)} %select_select_fusion.refs_0_, bf16[1024,192]{1,0:T(8,128)(2,1)} %bitcast.173), custom_call_target="tpu_custom_call" | custom-call | tf_op jit(solution)/shard_map/pallas_call | solution.py:166
  79.7 2.3 fusion.1
  82.0 2.3 convert_bitcast_fusion
  84.3 5.3 %copy.205 = f32[1024,4,192]{0,2,1:T(8,128)} copy(f32[1024,4,192]{2,0,1:T(8,128)} %convert_bitcast_fusion) | data formatting | bytes 6291456 | tf_op jit(solution)/shard_map/convert_element_type | solution.py:476
  89.5 2.4 %fusion.3 = bf16[1024,768]{0,1:T(8,128)(2,1)S(1)} fusion(f32[1024,4,192]{0,2,1:T(8,128)} %copy.205, f32[768]{0:T(1024)S(1)} %convert_element_type.208, f32[1024]{0:T(1024)S(1)} %add_rsqrt_fusion), kind=kLoop, calls=%fused_computation.6 | loop fusion | flops 2359296 | bytes 4725760 | tf_op jit(solution)/shard_map/convert_element_type | solution.py:478
  92.4 7.1 %shard_map.198 = (bf16[8,4,48,384]{3,2,1,0:T(8,128)(2,1)S(1)}, f32[768,768]{1,0:T(8,128)}, f32[768,768]{1,0:T(8,128)}) custom-call(bf16[8,48,768]{2,1,0:T(8,128)(2,1)S(1)} %copy-done.5, bf16[8,48,768]{2,1,0:T(8,128)(2,1)S(1)} %copy-done.4, bf16[768,768]{1,0:T(8,128)(2,1)S(1)} %bitcast.152, bf16[768,768]{1,0:T(8,128)(2,1)S(1)} %bitcast.153), custom_call_target="tpu_custom_call" | custom-call | tf_op jit(solution)/shard_map/pallas_call | solution.py:226
  99.5 1.0 copy-done.3
  100.5 32.3 %shard_map.199 = bf16[8,4,48,384]{3,2,1,0:T(8,128)(2,1)} custom-call(bf16[8,4,48,384]{3,2,1,0:T(8,128)(2,1)} %copy-done.3), custom_call_target="tpu_custom_call" | custom-call | tf_op jit(solution)/shard_map/pallas_call | solution.py:166
  132.8 2.7 %fusion.63 = f32[2,128,384]{2,1,0:T(8,128)} fusion(pred[2,128,1536]{2,1,0:T(32,128)(4,1)} %bitcast.178, bf16[1536,384,1]{1,0,2:T(8,128)(2,1)} %bitcast.168), kind=kOutput, calls=%fused_computation.172 | convolution fusion | flops 301989888 | bytes 1966080 | tf_op jit(solution)/shard_map/dot_general | solution.py:264
  135.5 1.0 add_reduce_fusion
  137.6 1.1 fusion.28
  138.7 1.7 slice_reduce_fusion.refs_0_
  141.2 5.3 %shard_map.200 = bf16[4,128,192]{2,1,0:T(8,128)(2,1)} custom-call(bf16[128,192]{1,0:T(8,128)(2,1)} %slice_reduce_fusion.refs_0_), custom_call_target="tpu_custom_call" | custom-call | tf_op jit(solution)/shard_map/pallas_call | solution.py:166
  146.5 1.8 convert_bitcast_fusion.1
  148.3 2.0 copy.187
  150.2 2.0 copy.188
  152.2 1.4 multiply_reduce_fusion.2
  153.6 1.1 multiply_subtract_fusion
  155.8 1.2 convolution_convert_fusion.3
  157.1 1.2 multiply_reduce_fusion.6
  159.1 1.0 multiply_reduce_fusion.1
  162.8 1.3 reshape.253
  164.1 1.0 slice_reduce_fusion.1
  165.1 0.8 convolution_convert_fusion.7
  167.6 1.1 copy.198
  169.9 0.9 copy.203
  170.8 33.5 %shard_map.201 = (bf16[8,128,576]{2,1,0:T(8,128)(2,1)}, bf16[8,16,768]{2,1,0:T(8,128)(2,1)}, bf16[4,128,256]{2,1,0:T(8,128)(2,1)}, bf16[8,96,192]{2,1,0:T(8,128)(2,1)}) custom-call(bf16[128,576]{1,0:T(8,128)(2,1)} %copy-done.10, bf16[16,768]{1,0:T(8,128)(2,1)} %pad.25.refs_1_, bf16[4,128,256]{2,1,0:T(8,128)(2,1)} %pad_maximum_fusion.1.refs_2_, ...), custom_call_target="tpu_custom_call" | custom-call | tf_op jit(solution)/shard_map/pallas_call | solution.py:166
  204.3 1.0 convert_reduce_fusion
  206.5 1.0 convert_reduce_fusion.1
  209.5 1.7 reduce_sum.252.refs_0_
  211.2 11.8 %shard_map.202 = (bf16[8,96,192]{2,1,0:T(8,128)(2,1)}, f32[4,8,768]{2,1,0:T(8,128)}) custom-call(bf16[96,192]{1,0:T(8,128)(2,1)} %reduce_sum.252.refs_0_, f32[8,768]{1,0:T(8,128)} %get-tuple-element.105.refs_1_), custom_call_target="tpu_custom_call" | custom-call | tf_op jit(solution)/shard_map/pallas_call | solution.py:166
  223.0 1.6 slice_reduce_fusion.2
  224.6 1.7 convolution_bitcast_fusion
  227.9 1.3 pad_maximum_fusion
  229.3 1.1 copy.206
  (171 shorter events, 27.4 us)
Async XLA Ops:
  0.6 1.2 copy-start
  7.3 5.1 %copy-start.12 = (bf16[128,192]{1,0:T(8,128)(2,1)}, bf16[128,192]{1,0:T(8,128)(2,1)S(1)}, u32[]{:S(2)}) copy-start(bf16[128,192]{1,0:T(8,128)(2,1)S(1)} %copy.172.refs_1_) | copy-start | bytes 147460
  28.9 3.8 %copy-start.27 = (f32[128]{0:T(128)}, f32[128]{0:T(128)S(1)}, u32[]{:S(2)}) copy-start(f32[128]{0:T(128)S(1)} %get-tuple-element.119) | copy-start | bytes 1540
  33.2 21.4 %copy-start.17 = (bf16[1,128,192]{1,2,0:T(8,128)(2,1)}, bf16[1,128,192]{1,2,0:T(8,128)(2,1)S(1)}, u32[]{:S(2)}) copy-start(bf16[1,128,192]{1,2,0:T(8,128)(2,1)S(1)} %get-tuple-element.101) | copy-start | bytes 147460
  33.2 21.4 %copy-start.19 = (bf16[1,128,192]{1,2,0:T(8,128)(2,1)}, bf16[1,128,192]{1,2,0:T(8,128)(2,1)S(1)}, u32[]{:S(2)}) copy-start(bf16[1,128,192]{1,2,0:T(8,128)(2,1)S(1)} %get-tuple-element.102) | copy-start | bytes 147460
  33.2 21.4 %copy-start.25 = (bf16[1,128,192]{1,2,0:T(8,128)(2,1)}, bf16[1,128,192]{1,2,0:T(8,128)(2,1)S(1)}, u32[]{:S(2)}) copy-start(bf16[1,128,192]{1,2,0:T(8,128)(2,1)S(1)} %get-tuple-element.103) | copy-start | bytes 147460
  33.5 21.2 %copy-start.15 = (f32[3,128,128]{1,2,0:T(8,128)}, f32[3,128,128]{1,2,0:T(8,128)S(1)}, u32[]{:S(2)}) copy-start(f32[3,128,128]{1,2,0:T(8,128)S(1)} %fusion.8) | copy-start | bytes 589828
  34.5 20.2 %copy-start.22 = (bf16[3,64,128]{2,1,0:T(8,128)(2,1)}, bf16[3,64,128]{2,1,0:T(8,128)(2,1)S(1)}, u32[]{:S(2)}) copy-start(bf16[3,64,128]{2,1,0:T(8,128)(2,1)S(1)} %convolution_convert_fusion.4) | copy-start | bytes 147460
  52.8 3.0 %copy-start.24 = (bf16[768,8]{0,1:T(8,128)(2,1)S(1)}, bf16[768,8]{0,1:T(8,128)(2,1)}, u32[]{:S(2)}) copy-start(bf16[768,8]{0,1:T(8,128)(2,1)} %param.19) | copy-start | bytes 36868
  52.8 3.3 %copy-start.26 = (s32[128,2]{0,1:T(2,128)S(1)}, s32[128,2]{0,1:T(2,128)}, u32[]{:S(2)}) copy-start(s32[128,2]{0,1:T(2,128)} %param.22) | copy-start | bytes 3076
  55.2 0.5 copy-start.30
  79.6 2.3 %copy-start.6 = (bf16[4,1024,192]{2,1,0:T(8,128)(2,1)S(1)}, bf16[4,1024,192]{2,1,0:T(8,128)(2,1)}, u32[]{:S(2)}) copy-start(bf16[4,1024,192]{2,1,0:T(8,128)(2,1)} %get-tuple-element.37) | copy-start | bytes 4718596
  89.5 2.4 %copy-start.1 = (bf16[1,768,768]{2,1,0:T(8,128)(2,1)S(1)}, bf16[1,768,768]{2,1,0:T(8,128)(2,1)}, u32[]{:S(2)}) copy-start(bf16[1,768,768]{2,1,0:T(8,128)(2,1)} %param.20) | copy-start | bytes 3538948
  89.5 2.6 %copy-start.2 = (bf16[1,768,768]{2,1,0:T(8,128)(2,1)S(1)}, bf16[1,768,768]{2,1,0:T(8,128)(2,1)}, u32[]{:S(2)}) copy-start(bf16[1,768,768]{2,1,0:T(8,128)(2,1)} %param.21) | copy-start | bytes 3538948
  89.5 2.7 %copy-start.4 = (bf16[8,48,768]{2,1,0:T(8,128)(2,1)S(1)}, bf16[8,48,768]{2,1,0:T(8,128)(2,1)}, u32[]{:S(2)}) copy-start(bf16[8,48,768]{2,1,0:T(8,128)(2,1)} %get-tuple-element.31.cot_ref) | copy-start | bytes 1769476
  89.5 2.9 %copy-start.5 = (bf16[8,48,768]{2,1,0:T(8,128)(2,1)S(1)}, bf16[8,48,768]{2,1,0:T(8,128)(2,1)}, u32[]{:S(2)}) copy-start(bf16[8,48,768]{2,1,0:T(8,128)(2,1)} %get-tuple-element.30.rows_ref) | copy-start | bytes 1769476
  99.5 1.0 copy-start.3
  150.2 5.2 %copy-start.11 = (bf16[192,768]{1,0:T(8,128)(2,1)S(1)}, bf16[192,768]{1,0:T(8,128)(2,1)}, u32[]{:S(2)}) copy-start(bf16[192,768]{1,0:T(8,128)(2,1)} %refs_1_.2) | copy-start | bytes 884740
  154.7 0.8 copy-start.7
  154.7 3.6 %copy-start.14 = (f32[3,128,128]{1,2,0:T(8,128)S(1)}, f32[3,128,128]{1,2,0:T(8,128)}, u32[]{:S(2)}) copy-start(f32[3,128,128]{1,2,0:T(8,128)} %get-tuple-element.125) | copy-start | bytes 589828
  154.8 3.6 %copy-start.20 = (bf16[1,128,192]{1,2,0:T(8,128)(2,1)S(1)}, bf16[1,128,192]{1,2,0:T(8,128)(2,1)}, u32[]{:S(2)}) copy-start(bf16[1,128,192]{1,2,0:T(8,128)(2,1)} %copy-done.19) | copy-start | bytes 147460
  155.5 3.1 %copy-start.18 = (bf16[1,128,192]{1,2,0:T(8,128)(2,1)S(1)}, bf16[1,128,192]{1,2,0:T(8,128)(2,1)}, u32[]{:S(2)}) copy-start(bf16[1,128,192]{1,2,0:T(8,128)(2,1)} %copy-done.17) | copy-start | bytes 147460
  155.7 3.4 %copy-start.28 = (f32[128]{0:T(128)S(1)}, f32[128]{0:T(128)}, u32[]{:S(2)}) copy-start(f32[128]{0:T(128)} %copy-done.27) | copy-start | bytes 1540
  158.4 2.6 %copy-start.33 = (bf16[64]{0:T(256)(128)(2,1)S(1)}, bf16[64]{0:T(256)(128)(2,1)}, u32[]{:S(2)}) copy-start(bf16[64]{0:T(256)(128)(2,1)} %pad.34.clone) | copy-start | bytes 388
  159.1 3.1 %copy-start.10 = (bf16[128,576]{1,0:T(8,128)(2,1)}, bf16[128,576]{1,0:T(8,128)(2,1)S(1)}, u32[]{:S(2)}) copy-start(bf16[128,576]{1,0:T(8,128)(2,1)S(1)} %pad_maximum_fusion.2.refs_0_) | copy-start | bytes 442372
  162.5 6.3 %copy-start.16 = (bf16[4,128,64]{2,1,0:T(8,128)(2,1)S(1)}, bf16[4,128,64]{2,1,0:T(8,128)(2,1)}, u32[]{:S(2)}) copy-start(bf16[4,128,64]{2,1,0:T(8,128)(2,1)} %broadcast_in_dim.176) | copy-start | bytes 196612
  162.8 6.8 %copy-start.8 = (f32[128,768]{1,0:T(8,128)S(1)}, f32[128,768]{1,0:T(8,128)}, u32[]{:S(2)}) copy-start(f32[128,768]{1,0:T(8,128)} %copy-done.7) | copy-start | bytes 1179652
  162.8 6.8 %copy-start.23 = (bf16[3,64,128]{2,1,0:T(8,128)(2,1)S(1)}, bf16[3,64,128]{2,1,0:T(8,128)(2,1)}, u32[]{:S(2)}) copy-start(bf16[3,64,128]{2,1,0:T(8,128)(2,1)} %copy-done.22) | copy-start | bytes 147460
  168.8 36.7 %copy-start.13 = (bf16[128,192]{1,0:T(8,128)(2,1)S(1)}, bf16[128,192]{1,0:T(8,128)(2,1)}, u32[]{:S(2)}) copy-start(bf16[128,192]{1,0:T(8,128)(2,1)} %copy-done.12) | copy-start | bytes 147460
  168.8 36.7 %copy-start.29 = (f32[128]{0:T(128)S(1)}, f32[128]{0:T(128)}, u32[]{:S(2)}) copy-start(f32[128]{0:T(128)} %copy-done.27) | copy-start | bytes 1540
  168.8 36.7 %copy-start.31 = (f32[192]{0:T(256)S(1)}, f32[192]{0:T(256)}, u32[]{:S(2)}) copy-start(f32[192]{0:T(256)} %dynamic_slice.11) | copy-start | bytes 2308
  168.8 36.7 %copy-start.34 = (f32[128]{0:T(128)S(1)}, f32[128]{0:T(128)}, u32[]{:S(2)}) copy-start(f32[128]{0:T(128)} %get-tuple-element.118) | copy-start | bytes 1540
  169.9 38.2 %copy-start.32 = (pred[8]{0:T(512)(128)(4,1)S(1)}, pred[8]{0:T(512)(128)(4,1)}, u32[]{:S(2)}) copy-start(pred[8]{0:T(512)(128)(4,1)} %constant.72.clone.1) | copy-start | bytes 28
  223.0 3.3 %copy-start.9 = (bf16[8,128,576]{2,1,0:T(8,128)(2,1)S(1)}, bf16[8,128,576]{2,1,0:T(8,128)(2,1)}, u32[]{:S(2)}) copy-start(bf16[8,128,576]{2,1,0:T(8,128)(2,1)} %get-tuple-element.38) | copy-start | bytes 3538948
  227.9 1.3 copy-start.21
